TPU v7x, 512 devices: a whole 4x8x8 slice. The times are simulated.
512 devices in a mesh: row: 16 (over x, z_hi, core), col: 32 (over y, z_lo).
Axes of the slice: x: 4, y: 8, z: 8 (z_hi: 2, z_lo: 4; z = z_hi * 4 + z_lo), core: 2. Of those that a mesh axis runs over, the one named last changes fastest.
Arguments:
- features: bfloat16 [65536, 128], P(('row', 'col')), may hold values from -6 to 6
- cotangent: bfloat16 [65536, 128], P(('row', 'col')), may hold values from -6 to 6
- self_weight: bfloat16 [128, 128], replicated, may hold values from -0.5 to 0.5
- neighbour_weight: bfloat16 [128, 128], replicated, may hold values from -0.5 to 0.5
- shift_bias: float32 [128], replicated, may hold values from -3 to 3
- tile_rows: int32 [16, 32, 128], P('row', 'col'), may hold values from 0 to 31, as said below
- tile_cols: int32 [16, 32, 128], P('row', 'col'), may hold values from 0 to 15
- edge_targets: int32 [16, 32, 128, 128], P('row', 'col'), may hold values from -1 to 127, as said below
- edge_sources: int32 [16, 32, 128, 128], P('row', 'col'), may hold values from -1 to 127
Outputs:
- activations: bfloat16 [65536, 128], P(('row', 'col'))
- feature_grad: bfloat16 [65536, 128], P(('row', 'col'))
- self_grad: float32 [128, 128], replicated
- neighbour_grad: float32 [128, 128], replicated
- bias_grad: float32 [128], replicated
Inputs may be any that keep to these rules, and one draw needn't show every extreme that they name: `tile_rows`: each device has 128 block slots; the live ones come first, at least one per device, and on some device all 128 are live. Live counts differ strongly from device to device. A live slot holds 1 to 128 edges in its first positions, the rest -1; some slot holds exactly 128; an empty slot is all -1. edge_sources is -1 exactly where edge_targets is.
All inputs are finite; a program needn't handle non-finite values.
Results may differ from a plain program's by a relative error of at most 0.0075.
Values may be sent and summed in bfloat16 or wider, within the bound.
A program may use at most 64 MiB of HBM per device.

v0:
```python
import jax
import jax.numpy as jnp
from jax import lax
from jax.sharding import PartitionSpec as P

TILE = 128


def build_blocks(targets, sources):
    positions = lax.broadcasted_iota(jnp.int32, (1, 1, TILE), 2)
    target_hot = (targets[..., None] == positions).astype(jnp.bfloat16)
    source_hot = (sources[..., None] == positions).astype(jnp.bfloat16)
    blocks = jnp.einsum("gei,gej->gij", target_hot, source_hot, preferred_element_type=jnp.float32)
    return blocks.astype(jnp.bfloat16)


def on_device(
    features,
    cotangent,
    self_weight,
    neighbour_weight,
    shift_bias,
    tile_rows,
    tile_cols,
    edge_targets,
    edge_sources,
):
    rows_dev, width = features.shape
    n_row = lax.axis_size("row")
    n_col = lax.axis_size("col")
    slot_count = edge_targets.shape[2]
    group = 8
    turns = slot_count // group
    target_groups = edge_targets.reshape(turns, group, -1)
    source_groups = edge_sources.reshape(turns, group, -1)
    row_groups = tile_rows.reshape(turns, group)
    col_groups = tile_cols.reshape(turns, group)
    self_term = jnp.dot(features, self_weight, preferred_element_type=jnp.float32)
    source_block = lax.all_gather(features, "row", axis=0, tiled=True).reshape(-1, TILE, width)

    def forward_step(carry, item):
        totals, counts = carry
        targets, sources, row_ids, col_ids = item
        blocks = build_blocks(targets, sources)
        picked = jnp.take(source_block, col_ids, axis=0)
        product = jnp.einsum("gij,gjf->gif", blocks, picked, preferred_element_type=jnp.float32)
        totals = totals.at[row_ids].add(product)
        counts = counts.at[row_ids].add(jnp.sum(blocks, axis=2, dtype=jnp.float32))
        return ((totals, counts), None)

    dest_tiles = n_col * rows_dev // TILE
    start_totals = jnp.zeros((dest_tiles, TILE, width), jnp.float32)
    start_counts = jnp.zeros((dest_tiles, TILE), jnp.float32)
    (totals, counts), _ = lax.scan(
        forward_step,
        (start_totals, start_counts),
        (target_groups, source_groups, row_groups, col_groups),
    )
    totals = totals.reshape(-1, width)
    counts = counts.reshape(-1)
    own_sum, degree = (
        lax.psum_scatter(totals, "col", scatter_dimension=0, tiled=True),
        lax.psum_scatter(counts, "col", scatter_dimension=0, tiled=True),
    )
    divisor = (degree + 1.0)[:, None]
    aggregate = (own_sum / divisor).astype(jnp.bfloat16)
    preact = (
        self_term
        + jnp.dot(aggregate, neighbour_weight, preferred_element_type=jnp.float32)
        + shift_bias
    )
    sigma = jax.nn.sigmoid(preact)
    activations = (preact * sigma).astype(jnp.bfloat16)
    grad_pre = (cotangent.astype(jnp.float32) * sigma * (1.0 + preact * (1.0 - sigma))).astype(
        jnp.bfloat16
    )
    contract_rows = (((0,), (0,)), ((), ()))
    self_local = lax.dot_general(
        features, grad_pre, contract_rows, preferred_element_type=jnp.float32
    )
    neighbour_local = lax.dot_general(
        aggregate, grad_pre, contract_rows, preferred_element_type=jnp.float32
    )
    bias_local = jnp.sum(grad_pre.astype(jnp.float32), axis=0)
    contract_cols = (((1,), (1,)), ((), ()))
    scaled_grad = (
        lax.dot_general(
            grad_pre, neighbour_weight, contract_cols, preferred_element_type=jnp.float32
        )
        / divisor
    ).astype(jnp.bfloat16)
    own_term = lax.dot_general(
        grad_pre, self_weight, contract_cols, preferred_element_type=jnp.float32
    )
    target_block = lax.all_gather(scaled_grad, "col", axis=0, tiled=True).reshape(-1, TILE, width)

    def backward_step(carry, item):
        targets, sources, row_ids, col_ids = item
        blocks = build_blocks(targets, sources)
        picked = jnp.take(target_block, row_ids, axis=0)
        product = jnp.einsum("gij,gif->gjf", blocks, picked, preferred_element_type=jnp.float32)
        return (carry.at[col_ids].add(product), None)

    source_tiles = n_row * rows_dev // TILE
    back_start = jnp.zeros((source_tiles, TILE, width), jnp.float32)
    back_totals, _ = lax.scan(
        backward_step, back_start, (target_groups, source_groups, row_groups, col_groups)
    )
    back_totals = back_totals.reshape(-1, width)
    back_own = lax.psum_scatter(back_totals, "row", scatter_dimension=0, tiled=True)
    feature_grad = (own_term + back_own).astype(jnp.bfloat16)
    self_sum, neighbour_sum, bias_sum = lax.psum(
        (self_local, neighbour_local, bias_local), ("row", "col")
    )
    scaling = (rows_dev * n_row * n_col) ** (-0.5)
    return (
        activations,
        feature_grad,
        self_sum * scaling,
        neighbour_sum * scaling,
        bias_sum * scaling,
    )


def solution(mesh):
    in_specs = (
        P(("row", "col"), None),
        P(("row", "col"), None),
        P(),
        P(),
        P(),
        P("row", "col", None),
        P("row", "col", None),
        P("row", "col", None, None),
        P("row", "col", None, None),
    )
    out_specs = (P(("row", "col"), None), P(("row", "col"), None), P(), P(), P())
    return jax.shard_map(
        on_device, mesh=mesh, in_specs=in_specs, out_specs=out_specs, check_vma=False
    )
```

profile of v0, /device:TPU:1, one launch (start us, length us, event | category | flops | bytes accessed | tf_op | source)
XLA Modules:
  0.0 806.9 jit_solution(12586704835713867157)
XLA Ops:
  10.6 40.7 %all_gather.6 = bf16[2048,128]{1,0:T(8,128)(2,1)} all-gather(bf16[128,128]{1,0:T(8,128)(2,1)} %param.13), channel_id=1, replica_groups=mesh['row'=16,'col'=32] {'row'}, dimensions={0}, use_global_device_ids=true | all-gather | bytes 557056 | tf_op jit(solution)/shard_map/all_gather | solution.py:39
  51.5 76.9 %while.22 = (s32[]{:T(128)}, f32[32,128,128]{2,1,0:T(8,128)S(1)}, f32[32,128]{1,0:T(8,128)S(1)}, s32[16,8]{1,0:T(8,128)S(1)}, s32[16,8,128]{2,1,0:T(8,128)}, /*i...) while((s32[]{:T(128)}, f32[32,128,128]{2,1,0:T(8,128)S(1)}, ...), condition=%wide.region_4.5_spmd, body=%wide.region_0.4_spmd.sunk | while | flops 68027488 | bytes 3453337 | solution.py:54
  131.8 128.5 %all-reduce = f32[4096]{0:T(1024)S(1)} all-reduce(f32[4096]{0:T(1024)S(1)} %bitcast.77), channel_id=3, replica_groups=mesh['row'=16,'col'=32] {'col'}, use_global_device_ids=true, to_apply=%region_6.7.clone | all-reduce | flops 4096 | bytes 32768
  260.5 7.5 reduce-scatter.3.cloned.1.call-done
  273.2 149.7 %all-gather.2.cloned.1.call-done = bf16[4096,128]{1,0:T(8,128)(2,1)} async-done(((bf16[128,128]{1,0:T(8,128)(2,1)}), bf16[4096,128]{1,0:T(8,128)(2,1)}) %all-gather.2.cloned.1.call-update) | async-done | bytes 1048592 | tf_op jit(solution)/shard_map/all_gather | solution.py:95
  422.9 67.6 %while.23 = (s32[]{:T(128)}, f32[16,128,128]{2,1,0:T(8,128)S(1)}, s32[16,8]{1,0:T(8,128)S(1)}, s32[16,8,128]{2,1,0:T(8,128)}, s32[16,8,128]{2,1,0:T(8,128)}, /*i...) while((s32[]{:T(128)}, f32[16,128,128]{2,1,0:T(8,128)S(1)}, s32[16,8]{1,0:T(8,128)S(1)}, ...), condition=%wide.region_9.10_spmd, body=%wide.region_7.9_spmd.sunk | while | flops 67765344 | bytes 2912625 | solution.py:106
  423.0 1.8 gather_fusion.1
  427.2 1.8 gather_fusion.1
  431.4 1.8 gather_fusion.1
  435.7 1.8 gather_fusion.1
  439.9 1.8 gather_fusion.1
  444.1 1.8 gather_fusion.1
  448.4 1.8 gather_fusion.1
  452.6 1.8 gather_fusion.1
  456.8 1.8 gather_fusion.1
  461.0 1.8 gather_fusion.1
  465.3 1.8 gather_fusion.1
  469.5 1.8 gather_fusion.1
  473.7 1.8 gather_fusion.1
  477.9 1.8 gather_fusion.1
  486.4 1.8 gather_fusion.1
  491.6 118.5 %psum.23 = f32[128]{0:T(128)S(1)} all-reduce(f32[128]{0:T(128)S(1)} %get-tuple-element.135), channel_id=1, replica_groups=mesh['row'=16,'col'=32] {'row','col'}, use_global_device_ids=true, to_apply=%region_14.15 | all-reduce | flops 128 | bytes 1024 | tf_op jit(solution)/shard_map/psum | solution.py:112
  610.6 103.5 %all-reduce.4.cloned.1.call-done = (f32[128,128]{0,1:T(8,128)}, f32[128,128]{0,1:T(8,128)}) async-done(((f32[128,128]{0,1:T(8,128)}, f32[128,128]{0,1:T(8,128)}), (f32[128,128]{0,1:T(8,128)}, f32[128,128]{0,1:T(8,128)})) %all-reduce.4.cloned.1.call-update) | async-done | bytes 131088 | tf_op jit(solution)/shard_map/psum | solution.py:112
  716.4 82.4 %reduce-scatter.5.cloned.1.call-done = f32[128,128]{1,0:T(8,128)} async-done(((f32[2048,128]{1,0:T(8,128)}), f32[128,128]{1,0:T(8,128)}) %reduce-scatter.5.cloned.1.call-update) | async-done | bytes 65552 | tf_op jit(solution)/shard_map/reduce_scatter | solution.py:110
  (283 shorter events, 132.5 us)
Async XLA Ops:
  7.2 260.9 %copy-start = (bf16[128,128]{1,0:T(8,128)(2,1)S(1)}, bf16[128,128]{1,0:T(8,128)(2,1)}, u32[]{:S(2)}) copy-start(bf16[128,128]{1,0:T(8,128)(2,1)} %param.16) | copy-start | bytes 98308
  7.2 260.9 %reduce-scatter.3.cloned.1.call-start = ((), (), s32[]{:S(2)}) async-start(), calls=%async_computation.2 | async-start | bytes 2162688 | tf_op jit(solution)/shard_map/reduce_scatter | solution.py:62
  128.4 1.4 copy-start.1
  128.4 132.0 %copy-start.3 = (bf16[128,128]{1,0:T(8,128)(2,1)S(1)}, bf16[128,128]{1,0:T(8,128)(2,1)}, u32[]{:S(2)}) copy-start(bf16[128,128]{1,0:T(8,128)(2,1)} %param.13) | copy-start | bytes 98308
  128.4 131.9 %copy-start.4 = (bf16[128,128]{1,0:T(8,128)(2,1)S(1)}, bf16[128,128]{1,0:T(8,128)(2,1)}, u32[]{:S(2)}) copy-start(bf16[128,128]{1,0:T(8,128)(2,1)} %param.15) | copy-start | bytes 98308
  128.4 139.6 %copy-start.5 = (bf16[128,128]{1,0:T(8,128)(2,1)S(1)}, bf16[128,128]{1,0:T(8,128)(2,1)}, u32[]{:S(2)}) copy-start(bf16[128,128]{1,0:T(8,128)(2,1)} %param.14) | copy-start | bytes 98308
  128.5 139.6 %copy-start.6 = (f32[128]{0:T(128)S(1)}, f32[128]{0:T(128)}, u32[]{:S(2)}) copy-start(f32[128]{0:T(128)} %param.17) | copy-start | bytes 1540
  129.8 293.1 %all-gather.2.cloned.1.call-start = ((), (), s32[]{:S(2)}) async-start(), calls=%async_computation.3 | async-start | bytes 1081344 | tf_op jit(solution)/shard_map/all_gather | solution.py:95
  270.5 443.5 %all-reduce.4.cloned.1.call-start = ((), (), s32[]{:S(2)}) async-start(), calls=%async_computation.5 | async-start | bytes 262144 | tf_op jit(solution)/shard_map/psum | solution.py:112
  273.1 525.6 %reduce-scatter.5.cloned.1.call-start = ((), (), s32[]{:S(2)}) async-start(), calls=%async_computation.4 | async-start | bytes 1114112 | tf_op jit(solution)/shard_map/reduce_scatter | solution.py:110
  490.6 1.0 copy-start.2
Sparse Core Ops, SparseCore 0:
  129.9 138.0 reduce-scatter.2
  270.9 151.9 all-gather.1
  429.5 284.4 all-reduce.3
  718.6 80.1 reduce-scatter.4
where the time goes:
time: 811 us; the launch traced here: 807 us
  waiting for transfers between devices  343 us (42%)
  blocking collectives  288 us (36%)
  local copies, waits for them, and re-layouts  84.2 us (10%)
  other arithmetic  48.5 us (6%)
  matrix products  27 us (3%)
  between operations  14.5 us (2%)
    all_gather x1, waiting for transfers between devices, on_device(): lax.all_gather(scaled_grad, 'col', axis=0, tiled=True)  150 us
    unnamed x1, blocking collectives  129 us
    psum x1, blocking collectives, on_device(): lax.psum((self_local, neighbour_local, bias_local), ('row', 'col'))  118 us
    psum x1, waiting for transfers between devices, on_device(): lax.psum((self_local, neighbour_local, bias_local), ('row', 'col'))  103 us
    reduce_scatter x1, waiting for transfers between devices, on_device(): lax.psum_scatter(back_totals, 'row', scatter_dimension=0, tiled=True)  82.4 us
    all_gather x1, blocking collectives, on_device(): lax.all_gather(features, 'row', axis=0, tiled=True).reshape(-1, TILE, width)  40.7 us
    gather x16, local copies, waits for them, and re-layouts, backward_step(): picked = jnp.take(target_block, row_ids, axis=0)  29.2 us
    gather x16, local copies, waits for them, and re-layouts, forward_step(): picked = jnp.take(source_block, col_ids, axis=0)  26.2 us
  transfers between devices with their start and end apart: 4, of which 4 were waited for; matrix products, arithmetic and copies ran while one was open for 9% of the time, Pallas kernels for 0%

commit v1 on v0

v1 whole, which is shorter than its diff:
```python
import functools

import jax
import jax.numpy as jnp
from jax import lax
from jax.experimental import pallas as pl
from jax.experimental.pallas import tpu as pltpu
from jax.sharding import PartitionSpec as P

TILE = 128
HALF = TILE // 2
CORES = 2
UNROLL = 8
MESH = pl.DeviceIdType.MESH
F32 = jnp.float32
BF16 = jnp.bfloat16
LANES = (((1,), (1,)), ((), ()))
ROWS = (((0,), (0,)), ((), ()))


def far_first(n):
    return sorted(range(1, n), key=lambda d: -min(d, n - d))


def layer_kernel(
    sizes,
    feat,
    cot,
    ws,
    wn,
    bias,
    trow,
    tcol,
    et,
    es,
    act_o,
    fg_o,
    sg_o,
    ng_o,
    bg_o,
    fwd_adj,
    bwd_adj,
    runs,
    slot_counts,
    meta_v,
    meta_s,
    xb,
    pa,
    pb,
    ra,
    rb,
    sa,
    sb,
    ra2,
    rb2,
    deg,
    deg_r,
    deg2,
    deg2_r,
    ga,
    gb,
    bp,
    br,
    bs,
    br2,
    wl,
    wc,
    w1,
    wx,
    w2,
    wy,
    w3,
    wz,
    wo,
    send_sems,
    recv_sems,
    meta_sem,
):
    n_q, n_y, n_z, slots, scaling = sizes
    r = lax.axis_index("row")
    c = lax.axis_index("col")
    q, k = r // CORES, r % CORES
    y, z = c // n_z, c % n_z
    n_src = n_q * CORES
    n_dst = n_y * n_z
    wrows = TILE // n_q

    def at_y(d):
        return (r, lax.rem(y + d, n_y) * n_z + z)

    def at_z(d):
        return (r, y * n_z + lax.rem(z + d, n_z))

    def at_q(d):
        return (lax.rem(q + d, n_q) * CORES + k, c)

    sibling = (q * CORES + 1 - k, c)

    used = [0]
    started = []

    def send(src, dst, device):
        i = used[0]
        used[0] += 1
        copy = pltpu.make_async_remote_copy(
            src_ref=src,
            dst_ref=dst,
            send_sem=send_sems.at[i],
            recv_sem=recv_sems.at[i],
            device_id=device,
            device_id_type=MESH,
        )
        copy.start()
        started.append(copy)
        return copy

    def arrive(copies):
        for copy in copies:
            copy.wait_recv()

    y_far, z_far, q_far = far_first(n_y), far_first(n_z), far_first(n_q)

    barrier = pltpu.get_barrier_semaphore()
    partners = [at_y(d) for d in y_far] + [at_z(d) for d in z_far]
    partners += [at_q(d) for d in q_far] + [sibling]
    for partner in partners:
        pl.semaphore_signal(barrier, inc=1, device_id=partner, device_id_type=MESH)

    sub = lax.broadcasted_iota(jnp.int32, (TILE, TILE), 0)
    lane = lax.broadcasted_iota(jnp.int32, (TILE, TILE), 1)
    rows_l = jnp.broadcast_to(trow[...], (TILE, TILE))
    cols_l = jnp.broadcast_to(tcol[...], (TILE, TILE))
    rows_s, cols_s = rows_l.T, cols_l.T

    def order(ids_l, ids_s, other_s):
        before = (ids_l < ids_s) | ((ids_l == ids_s) & (lane < sub))
        rank = jnp.sum(before.astype(jnp.int32), axis=1, keepdims=True)
        same = jnp.sum(((ids_l == ids_s) & (lane < sub)).astype(jnp.int32), axis=1, keepdims=True)
        packed = sub + other_s * 128 + jnp.minimum(same, 1) * 4096
        ordered = jnp.sum(jnp.where(rank == lane, packed, 0), axis=0, keepdims=True)
        upto = jnp.sum((ids_s <= lane).astype(jnp.int32), axis=0, keepdims=True)
        below = jnp.sum((ids_s < lane).astype(jnp.int32), axis=0, keepdims=True)
        ends = jnp.maximum(upto - 1, 0) + jnp.where(upto > below, 256, 0)
        return ordered, ends

    by_row, row_ends = order(rows_l, rows_s, cols_s)
    by_col, col_ends = order(cols_l, cols_s, rows_s)
    zero_row = jnp.zeros_like(by_row)
    meta_v[...] = jnp.concatenate([by_row, row_ends, by_col, col_ends] + [zero_row] * 4, axis=0)
    meta_copy = pltpu.make_async_copy(meta_v, meta_s, meta_sem)
    meta_copy.start()

    def build(g, _):
        base = pl.multiple_of(g * UNROLL, UNROLL)
        targets = et[pl.ds(base, UNROLL), :]
        sources = es[pl.ds(base, UNROLL), :]
        counts = []
        for u in range(UNROLL):
            hot_t = jnp.where(sub == targets[u : u + 1, :], 1.0, 0.0).astype(BF16)
            hot_s = jnp.where(sub == sources[u : u + 1, :], 1.0, 0.0).astype(BF16)
            fwd = lax.dot_general(hot_t, hot_s, LANES, preferred_element_type=F32)
            bwd = lax.dot_general(hot_s, hot_t, LANES, preferred_element_type=F32)
            fwd_adj[base + u] = fwd.astype(BF16)
            bwd_adj[base + u] = bwd.astype(BF16)
            counts.append(jnp.sum(bwd, axis=0, keepdims=True))
        slot_counts[pl.ds(base, UNROLL), :] = jnp.concatenate(counts, axis=0)
        return 0

    lax.fori_loop(0, slots // UNROLL, build, 0)

    xb[k * n_q + q] = feat[...]
    pl.semaphore_wait(barrier, len(partners))

    mine = xb.at[k * n_q + q]
    x_copies = [send(mine, mine, at_q(d)) for d in q_far]

    tile_sub = lax.broadcasted_iota(jnp.int32, (n_y * 8, TILE), 0)
    wanted = (tile_sub // 8) * n_z + tile_sub % 8
    hits = (jnp.broadcast_to(trow[...], (n_y * 8, TILE)) == wanted) & (tile_sub % 8 < n_z)
    partial = jnp.dot(
        jnp.where(hits, 1.0, 0.0).astype(BF16),
        slot_counts[...].astype(BF16),
        preferred_element_type=F32,
    )
    deg[...] = partial.reshape(n_y, 8, TILE)
    deg_copies = [send(deg.at[lax.rem(y + d, n_y)], deg_r.at[d], at_y(d)) for d in y_far]
    self_term = jnp.dot(feat[...], ws[...], preferred_element_type=F32)

    meta_copy.wait()
    arrive(x_copies)
    half_block = xb.at[pl.ds(k * n_q, n_q)]
    x_core = send(half_block, half_block, sibling)
    arrive(deg_copies)
    summed = deg[y]
    for d in range(1, n_y):
        summed = summed + deg_r[d]
    deg2[...] = summed
    deg2_copies = [send(deg2, deg2_r.at[d], at_z(d)) for d in z_far]
    arrive([x_core])

    def forward(g, acc):
        for u in range(UNROLL):
            s = g * UNROLL + u
            word = meta_s[0, s]
            slot, col = word & 127, (word >> 7) & 31
            source = xb[(col & 1) * n_q + (col >> 1)]
            product = jnp.dot(fwd_adj[slot], source, preferred_element_type=F32)
            acc = jnp.where(word >= 4096, acc, 0.0) + product
            runs[s] = acc.astype(BF16)
        return acc

    lax.fori_loop(0, slots // UNROLL, forward, jnp.zeros((TILE, TILE), F32))

    def place_rows(i, _):
        word = meta_s[1, i]
        run = runs[word & 127]
        run = jnp.where(word >= 256, run, jnp.zeros_like(run))
        pa[i] = run[:HALF]
        pb[(i % n_z) * n_y + i // n_z] = run[HALF:]
        return 0

    lax.fori_loop(0, n_dst, place_rows, 0)

    a_copies = [
        send(pa.at[pl.ds(lax.rem(y + d, n_y) * n_z, n_z)], ra.at[d], at_y(d)) for d in y_far
    ]
    b_copies = [
        send(pb.at[pl.ds(lax.rem(z + d, n_z) * n_y, n_y)], rb.at[d], at_z(d)) for d in z_far
    ]

    arrive(deg2_copies)
    degree = deg2[...]
    for d in range(1, n_z):
        degree = degree + deg2_r[d]
    sub8 = lax.broadcasted_iota(jnp.int32, (8, TILE), 0)
    degree = jnp.sum(jnp.where(sub8 == z, degree, 0.0), axis=0, keepdims=True)
    inverse = 1.0 / (jnp.broadcast_to(degree, (TILE, TILE)).T + 1.0)

    arrive(a_copies)
    total = pa[pl.ds(y * n_z, n_z)].astype(F32)
    for d in range(1, n_y):
        total = total + ra[d].astype(F32)
    sa[...] = total.astype(BF16)
    a2_copies = [send(sa.at[lax.rem(z + d, n_z)], ra2.at[d], at_z(d)) for d in z_far]
    arrive(b_copies)
    total = pb[pl.ds(z * n_y, n_y)].astype(F32)
    for d in range(1, n_z):
        total = total + rb[d].astype(F32)
    sb[...] = total.astype(BF16)
    b2_copies = [send(sb.at[lax.rem(y + d, n_y)], rb2.at[d], at_y(d)) for d in y_far]
    arrive(a2_copies)
    upper = sa[z].astype(F32)
    for d in range(1, n_z):
        upper = upper + ra2[d].astype(F32)
    arrive(b2_copies)
    lower = sb[y].astype(F32)
    for d in range(1, n_y):
        lower = lower + rb2[d].astype(F32)
    neighbour_sum = jnp.concatenate([upper, lower], axis=0)

    aggregate = (neighbour_sum * inverse).astype(BF16)
    preact = self_term + jnp.dot(aggregate, wn[...], preferred_element_type=F32) + bias[...]
    sigma = jax.nn.sigmoid(preact)
    grad_pre = (cot[...].astype(F32) * sigma * (1.0 + preact * (1.0 - sigma))).astype(BF16)
    scaled = lax.dot_general(grad_pre, wn[...], LANES, preferred_element_type=F32) * inverse
    scaled = scaled.astype(BF16)

    ga[y * n_z + z] = scaled[:HALF]
    gb[z * n_y + y] = scaled[HALF:]
    own_a, own_b = ga.at[y * n_z + z], gb.at[z * n_y + y]
    b_copies = [send(own_b, own_b, at_y(d)) for d in y_far]
    a_copies = [send(own_a, own_a, at_z(d)) for d in z_far]

    act_o[...] = (preact * sigma).astype(BF16)
    self_local = lax.dot_general(feat[...], grad_pre, ROWS, preferred_element_type=F32)
    neighbour_local = lax.dot_general(aggregate, grad_pre, ROWS, preferred_element_type=F32)
    bias_local = jnp.sum(grad_pre.astype(F32).reshape(TILE // 8, 8, TILE), axis=0)
    wl[0, :TILE] = self_local
    wl[1, :TILE] = neighbour_local
    wl[0, TILE:] = bias_local
    wl[1, TILE:] = bias_local
    own_term = lax.dot_general(grad_pre, ws[...], LANES, preferred_element_type=F32)
    w_core = send(wl.at[1 - k], wc, sibling)

    arrive(a_copies)
    group_a = ga.at[pl.ds(y * n_z, n_z)]
    a_copies = [send(group_a, group_a, at_y(d)) for d in y_far]
    arrive(b_copies)
    group_b = gb.at[pl.ds(z * n_y, n_y)]
    b_copies = [send(group_b, group_b, at_z(d)) for d in z_far]

    arrive([w_core])
    both = wl[k] + wc[...]
    for j in range(n_q):
        w1[j] = jnp.concatenate([both[j * wrows : (j + 1) * wrows], both[TILE:]], axis=0)
    wx_copies = [send(w1.at[lax.rem(q + d, n_q)], wx.at[d], at_q(d)) for d in q_far]
    arrive(wx_copies)
    summed = w1[q]
    for d in range(1, n_q):
        summed = summed + wx[d]
    w2[...] = summed
    wy_copies = [send(w2, wy.at[d], at_y(d)) for d in y_far]

    arrive(a_copies)
    arrive(b_copies)

    def backward(g, acc):
        for u in range(UNROLL):
            s = g * UNROLL + u
            word = meta_s[2, s]
            slot, row = word & 127, (word >> 7) & 31
            target = jnp.concatenate([ga[row], gb[(row % n_z) * n_y + row // n_z]], axis=0)
            product = jnp.dot(bwd_adj[slot], target, preferred_element_type=F32)
            acc = jnp.where(word >= 4096, acc, 0.0) + product
            runs[s] = acc.astype(BF16)
        return acc

    lax.fori_loop(0, slots // UNROLL, backward, jnp.zeros((TILE, TILE), F32))

    def place_cols(j, _):
        word = meta_s[3, j]
        run = runs[word & 127]
        run = jnp.where(word >= 256, run, jnp.zeros_like(run))
        bp[(j % CORES) * n_q + j // CORES] = run
        return 0

    lax.fori_loop(0, n_src, place_cols, 0)

    b_core = send(bp.at[pl.ds((1 - k) * n_q, n_q)], br, sibling)
    arrive(wy_copies)
    summed = w2[...]
    for d in range(1, n_y):
        summed = summed + wy[d]
    w3[...] = summed
    wz_copies = [send(w3, wz.at[d], at_z(d)) for d in z_far]
    arrive([b_core])
    bs[...] = (bp[pl.ds(k * n_q, n_q)].astype(F32) + br[...].astype(F32)).astype(BF16)
    back_copies = [send(bs.at[lax.rem(q + d, n_q)], br2.at[d], at_q(d)) for d in q_far]

    arrive(wz_copies)
    summed = w3[...]
    for d in range(1, n_z):
        summed = summed + wz[d]
    summed = summed * scaling
    bg_o[...] = jnp.sum(summed[wrows:], axis=0, keepdims=True)
    wo[k * n_q + q] = summed[:wrows]
    own_w = wo.at[k * n_q + q]
    wo_copies = [send(own_w, own_w, at_q(d)) for d in q_far]

    arrive(back_copies)
    feature_grad = own_term + bs[q].astype(F32)
    for d in range(1, n_q):
        feature_grad = feature_grad + br2[d].astype(F32)
    fg_o[...] = feature_grad.astype(BF16)

    arrive(wo_copies)
    own_half = wo.at[pl.ds(k * n_q, n_q)]
    arrive([send(own_half, own_half, sibling)])
    sg_o[...] = wo[pl.ds(0, n_q)].reshape(TILE, TILE)
    ng_o[...] = wo[pl.ds(n_q, n_q)].reshape(TILE, TILE)
    for copy in started:
        copy.wait_send()


def on_device(
    n_row,
    n_col,
    features,
    cotangent,
    self_weight,
    neighbour_weight,
    shift_bias,
    tile_rows,
    tile_cols,
    edge_targets,
    edge_sources,
):
    slots = edge_targets.shape[2]
    n_z = 4 if n_col >= 16 else 2
    n_y, n_q = n_col // n_z, n_row // CORES
    scaling = float((TILE * n_row * n_col) ** (-0.5))
    sizes = (n_q, n_y, n_z, slots, scaling)
    wrows = TILE // n_q
    n_dst, n_src = n_col, n_row
    copies = 7 * (n_y - 1) + 6 * (n_z - 1) + 4 * (n_q - 1) + 4
    scratch = [
        pltpu.VMEM((slots, TILE, TILE), BF16),
        pltpu.VMEM((slots, TILE, TILE), BF16),
        pltpu.VMEM((slots, TILE, TILE), BF16),
        pltpu.VMEM((slots, TILE), F32),
        pltpu.VMEM((8, TILE), jnp.int32),
        pltpu.SMEM((8, TILE), jnp.int32),
        pltpu.VMEM((n_src, TILE, TILE), BF16),
        pltpu.VMEM((n_dst, HALF, TILE), BF16),
        pltpu.VMEM((n_dst, HALF, TILE), BF16),
        pltpu.VMEM((n_y, n_z, HALF, TILE), BF16),
        pltpu.VMEM((n_z, n_y, HALF, TILE), BF16),
        pltpu.VMEM((n_z, HALF, TILE), BF16),
        pltpu.VMEM((n_y, HALF, TILE), BF16),
        pltpu.VMEM((n_z, HALF, TILE), BF16),
        pltpu.VMEM((n_y, HALF, TILE), BF16),
        pltpu.VMEM((n_y, 8, TILE), F32),
        pltpu.VMEM((n_y, 8, TILE), F32),
        pltpu.VMEM((8, TILE), F32),
        pltpu.VMEM((n_z, 8, TILE), F32),
        pltpu.VMEM((n_dst, HALF, TILE), BF16),
        pltpu.VMEM((n_dst, HALF, TILE), BF16),
        pltpu.VMEM((n_src, TILE, TILE), BF16),
        pltpu.VMEM((n_q, TILE, TILE), BF16),
        pltpu.VMEM((n_q, TILE, TILE), BF16),
        pltpu.VMEM((n_q, TILE, TILE), BF16),
        pltpu.VMEM((CORES, TILE + 8, TILE), F32),
        pltpu.VMEM((TILE + 8, TILE), F32),
        pltpu.VMEM((n_q, wrows + 8, TILE), F32),
        pltpu.VMEM((n_q, wrows + 8, TILE), F32),
        pltpu.VMEM((wrows + 8, TILE), F32),
        pltpu.VMEM((n_y, wrows + 8, TILE), F32),
        pltpu.VMEM((wrows + 8, TILE), F32),
        pltpu.VMEM((n_z, wrows + 8, TILE), F32),
        pltpu.VMEM((CORES * n_q, wrows, TILE), F32),
        pltpu.SemaphoreType.DMA((copies,)),
        pltpu.SemaphoreType.DMA((copies,)),
        pltpu.SemaphoreType.DMA,
    ]
    whole = pl.BlockSpec(memory_space=pltpu.VMEM)
    act, fg, sg, ng, bg = pl.pallas_call(
        functools.partial(layer_kernel, sizes),
        out_shape=(
            jax.ShapeDtypeStruct((TILE, TILE), BF16),
            jax.ShapeDtypeStruct((TILE, TILE), BF16),
            jax.ShapeDtypeStruct((TILE, TILE), F32),
            jax.ShapeDtypeStruct((TILE, TILE), F32),
            jax.ShapeDtypeStruct((1, TILE), F32),
        ),
        in_specs=[whole] * 9,
        out_specs=(whole,) * 5,
        scratch_shapes=scratch,
        compiler_params=pltpu.CompilerParams(
            collective_id=0, has_side_effects=True, vmem_limit_bytes=44 * 2**20
        ),
        name="sage_layer",
    )(
        features,
        cotangent,
        self_weight,
        neighbour_weight,
        shift_bias.reshape(1, TILE),
        tile_rows.reshape(1, slots),
        tile_cols.reshape(1, slots),
        edge_targets.reshape(slots, -1),
        edge_sources.reshape(slots, -1),
    )
    return act, fg, sg, ng, bg.reshape(TILE)


def solution(mesh):
    in_specs = (
        P(("row", "col"), None),
        P(("row", "col"), None),
        P(),
        P(),
        P(),
        P("row", "col", None),
        P("row", "col", None),
        P("row", "col", None, None),
        P("row", "col", None, None),
    )
    out_specs = (P(("row", "col"), None), P(("row", "col"), None), P(), P(), P())
    body = functools.partial(on_device, mesh.shape["row"], mesh.shape["col"])
    return jax.shard_map(
        body, mesh=mesh, in_specs=in_specs, out_specs=out_specs, check_vma=False
    )
```

time: 811 us -> 103 us (0.13)
  waiting for transfers between devices: 343 us -> 0 us
  blocking collectives: 288 us -> 0 us
  Pallas kernels: 0 us -> 93.3 us
  local copies, waits for them, and re-layouts: 84.2 us -> 8.37 us
  other arithmetic: 48.5 us -> 0 us
  matrix products: 27 us -> 0 us
  between operations: 14.5 us -> 0.68 us
    all_gather x1 -> x0, waiting for transfers between devices: 150 us -> none  [on_device(): lax.all_gather(scaled_grad, 'col', axis=0, tiled=True)]
    unnamed x1 -> x0, blocking collectives: 129 us -> none
    psum x1 -> x0, blocking collectives: 118 us -> none  [on_device(): lax.psum((self_local, neighbour_local, bias_local), ('row', 'col'))]
    psum x1 -> x0, waiting for transfers between devices: 103 us -> none  [on_device(): lax.psum((self_local, neighbour_local, bias_local), ('row', 'col'))]
    pallas_call x0 -> x1, Pallas kernels: none -> 93.3 us  [on_device(): pl.pallas_call(functools.partial(layer_kernel, sizes), out_shape=(jax.Sha...]
    reduce_scatter x2 -> x0, waiting for transfers between devices: 89.9 us -> none  [the longest x1 82.4 us: on_device(): lax.psum_scatter(back_totals, 'row', scatter_dimension=0, tiled=True)]
    gather x32 -> x0, local copies, waits for them, and re-layouts: 55.4 us -> none  [the longest x16 29.2 us: backward_step(): picked = jnp.take(target_block, row_ids, axis=0)]
    scatter-add x48 -> x0, other arithmetic: 43.4 us -> none  [the longest x16 16.6 us: backward_step(): return (carry.at[col_ids].add(product), None)]
  transfers between devices with their start and end apart: 4 -> 0, of which waited for: 4 -> 0; matrix products, arithmetic and copies ran while one was open for 9% -> 0% of each run, Pallas kernels for 0% -> 0%
where the time goes in v1:
time: 103 us; the launch traced here: 102 us
  Pallas kernels  93.3 us (91%)
  local copies, waits for them, and re-layouts  8.37 us (8%)
    pallas_call x1, Pallas kernels, on_device(): pl.pallas_call(functools.partial(layer_kernel, sizes), out_shape=(jax.Sha...  93.3 us
    unnamed x23, local copies, waits for them, and re-layouts  8.37 us

profile of v1, /device:TPU:1, one launch (start us, length us, event | category | flops | bytes accessed | tf_op | source)
XLA Modules:
  0.0 102.3 jit_solution(12301274156108317333)
XLA Ops:
  0.6 0.0 copy-start.6
  0.6 0.0 copy-start.7
  0.7 0.0 copy-start.8
  0.7 0.6 copy-done.6
  1.3 0.0 copy-done.7
  1.3 0.0 copy-done.8
  1.3 0.0 copy-start
  1.3 0.8 copy-done
  2.2 0.0 copy-start.1
  2.2 0.8 copy-done.1
  3.0 0.0 copy-start.2
  3.0 0.8 copy-done.2
  3.8 0.0 copy-start.3
  3.8 0.8 copy-done.3
  4.5 0.0 copy-start.4
  4.5 0.8 copy-done.4
  5.3 0.0 copy-start.5
  5.3 0.8 copy-done.5
  6.0 93.3 %sage_layer.1 = (bf16[128,128]{1,0:T(8,128)(2,1)S(1)}, bf16[128,128]{1,0:T(8,128)(2,1)S(1)}, f32[128,128]{1,0:T(8,128)S(1)}, f32[128,128]{1,0:T(8,128)S(1)}, f32[1,128]{1,0:T(1,128)S(1)}) custom-call(bf16[128,128]{1,0:T(8,128)(2,1)S(1)} %copy-done.2, bf16[128,128]{1,0:T(8,128)(2,1)S(1)} %copy-done.3, bf16[128,128]{1,0:T(8,128)(2,1)S(1)} %copy-done.4, ...), custom_call_target="tpu_custom_call" | custom-call | tf_op jit(solution)/shard_map/sage_layer/pallas_call | solution.py:426
  99.3 0.6 copy.19
  99.9 0.6 copy.20
  100.6 0.6 copy.21
  101.2 0.6 copy.22
  101.8 0.5 copy.23
Async XLA Ops:
  0.6 0.7 copy-start.6
  0.6 0.7 copy-start.7
  0.7 0.7 copy-start.8
  1.3 0.8 copy-start
  2.2 0.8 copy-start.1
  3.0 0.8 copy-start.2
  3.8 0.8 copy-start.3
  4.5 0.8 copy-start.4
  5.3 0.8 copy-start.5

commit v2 on v1

--- a/solution.py
+++ b/solution.py
@@ -24,6 +24,20 @@
 
 def layer_kernel(
     sizes,
+    feat_h,
+    cot_h,
+    ws_h,
+    wn_h,
+    bias_h,
+    trow_h,
+    tcol_h,
+    et_h,
+    es_h,
+    act_o,
+    fg_o,
+    sg_o,
+    ng_o,
+    bg_o,
     feat,
     cot,
     ws,
@@ -33,11 +47,9 @@
     tcol,
     et,
     es,
-    act_o,
-    fg_o,
-    sg_o,
-    ng_o,
-    bg_o,
+    act_v,
+    fg_v,
+    bg_v,
     fwd_adj,
     bwd_adj,
     runs,
@@ -75,6 +87,8 @@
     send_sems,
     recv_sems,
     meta_sem,
+    in_sems,
+    out_sems,
 ):
     n_q, n_y, n_z, slots, scaling = sizes
     r = lax.axis_index("row")
@@ -120,11 +134,31 @@
 
     y_far, z_far, q_far = far_first(n_y), far_first(n_z), far_first(n_q)
 
+    local_in = []
+    for i, (far, near) in enumerate(
+        zip(
+            (trow_h, tcol_h, feat_h, et_h, es_h, ws_h, wn_h, bias_h, cot_h),
+            (trow, tcol, feat, et, es, ws, wn, bias, cot),
+        )
+    ):
+        local_in.append(pltpu.make_async_copy(far, near, in_sems.at[i]))
+        local_in[-1].start()
+
+    local_out = []
+
+    def put(src, dst):
+        copy = pltpu.make_async_copy(src, dst, out_sems.at[len(local_out)])
+        copy.start()
+        local_out.append(copy)
+
     barrier = pltpu.get_barrier_semaphore()
     partners = [at_y(d) for d in y_far] + [at_z(d) for d in z_far]
     partners += [at_q(d) for d in q_far] + [sibling]
     for partner in partners:
         pl.semaphore_signal(barrier, inc=1, device_id=partner, device_id_type=MESH)
+
+    for copy in local_in[:2]:
+        copy.wait()
 
     sub = lax.broadcasted_iota(jnp.int32, (TILE, TILE), 0)
     lane = lax.broadcasted_iota(jnp.int32, (TILE, TILE), 1)
@@ -149,6 +183,16 @@
     meta_v[...] = jnp.concatenate([by_row, row_ends, by_col, col_ends] + [zero_row] * 4, axis=0)
     meta_copy = pltpu.make_async_copy(meta_v, meta_s, meta_sem)
     meta_copy.start()
+
+    local_in[2].wait()
+    xb[k * n_q + q] = feat[...]
+    pl.semaphore_wait(barrier, len(partners))
+
+    mine = xb.at[k * n_q + q]
+    x_copies = {d: send(mine, mine, at_q(d)) for d in q_far}
+    x_core = [send(mine, mine, sibling)]
+    for copy in local_in[3:]:
+        copy.wait()
 
     def build(g, _):
         base = pl.multiple_of(g * UNROLL, UNROLL)
@@ -168,12 +212,6 @@
 
     lax.fori_loop(0, slots // UNROLL, build, 0)
 
-    xb[k * n_q + q] = feat[...]
-    pl.semaphore_wait(barrier, len(partners))
-
-    mine = xb.at[k * n_q + q]
-    x_copies = [send(mine, mine, at_q(d)) for d in q_far]
-
     tile_sub = lax.broadcasted_iota(jnp.int32, (n_y * 8, TILE), 0)
     wanted = (tile_sub // 8) * n_z + tile_sub % 8
     hits = (jnp.broadcast_to(trow[...], (n_y * 8, TILE)) == wanted) & (tile_sub % 8 < n_z)
@@ -187,16 +225,11 @@
     self_term = jnp.dot(feat[...], ws[...], preferred_element_type=F32)
 
     meta_copy.wait()
-    arrive(x_copies)
-    half_block = xb.at[pl.ds(k * n_q, n_q)]
-    x_core = send(half_block, half_block, sibling)
-    arrive(deg_copies)
-    summed = deg[y]
-    for d in range(1, n_y):
-        summed = summed + deg_r[d]
-    deg2[...] = summed
-    deg2_copies = [send(deg2, deg2_r.at[d], at_z(d)) for d in z_far]
-    arrive([x_core])
+    for d in reversed(q_far):
+        arrive([x_copies[d]])
+        block = xb.at[k * n_q + lax.rem(q + n_q - d, n_q)]
+        x_core.append(send(block, block, sibling))
+    arrive(x_core)
 
     def forward(g, acc):
         for u in range(UNROLL):
@@ -228,6 +261,20 @@
         send(pb.at[pl.ds(lax.rem(z + d, n_z) * n_y, n_y)], rb.at[d], at_z(d)) for d in z_far
     ]
 
+    arrive(deg_copies)
+    summed = deg[y]
+    for d in range(1, n_y):
+        summed = summed + deg_r[d]
+    deg2[...] = summed
+    deg2_copies = [send(deg2, deg2_r.at[d], at_z(d)) for d in z_far]
+
+    arrive(a_copies)
+    total = pa[pl.ds(y * n_z, n_z)].astype(F32)
+    for d in range(1, n_y):
+        total = total + ra[d].astype(F32)
+    sa[...] = total.astype(BF16)
+    a2_copies = [send(sa.at[lax.rem(z + d, n_z)], ra2.at[d], at_z(d)) for d in z_far]
+
     arrive(deg2_copies)
     degree = deg2[...]
     for d in range(1, n_z):
@@ -236,12 +283,6 @@
     degree = jnp.sum(jnp.where(sub8 == z, degree, 0.0), axis=0, keepdims=True)
     inverse = 1.0 / (jnp.broadcast_to(degree, (TILE, TILE)).T + 1.0)
 
-    arrive(a_copies)
-    total = pa[pl.ds(y * n_z, n_z)].astype(F32)
-    for d in range(1, n_y):
-        total = total + ra[d].astype(F32)
-    sa[...] = total.astype(BF16)
-    a2_copies = [send(sa.at[lax.rem(z + d, n_z)], ra2.at[d], at_z(d)) for d in z_far]
     arrive(b_copies)
     total = pb[pl.ds(z * n_y, n_y)].astype(F32)
     for d in range(1, n_z):
@@ -271,7 +312,8 @@
     b_copies = [send(own_b, own_b, at_y(d)) for d in y_far]
     a_copies = [send(own_a, own_a, at_z(d)) for d in z_far]
 
-    act_o[...] = (preact * sigma).astype(BF16)
+    act_v[...] = (preact * sigma).astype(BF16)
+    put(act_v, act_o)
     self_local = lax.dot_general(feat[...], grad_pre, ROWS, preferred_element_type=F32)
     neighbour_local = lax.dot_general(aggregate, grad_pre, ROWS, preferred_element_type=F32)
     bias_local = jnp.sum(grad_pre.astype(F32).reshape(TILE // 8, 8, TILE), axis=0)
@@ -282,6 +324,12 @@
     own_term = lax.dot_general(grad_pre, ws[...], LANES, preferred_element_type=F32)
     w_core = send(wl.at[1 - k], wc, sibling)
 
+    arrive([w_core])
+    both = wl[k] + wc[...]
+    for j in range(n_q):
+        w1[j] = jnp.concatenate([both[j * wrows : (j + 1) * wrows], both[TILE:]], axis=0)
+    wx_copies = [send(w1.at[lax.rem(q + d, n_q)], wx.at[d], at_q(d)) for d in q_far]
+
     arrive(a_copies)
     group_a = ga.at[pl.ds(y * n_z, n_z)]
     a_copies = [send(group_a, group_a, at_y(d)) for d in y_far]
@@ -289,11 +337,6 @@
     group_b = gb.at[pl.ds(z * n_y, n_y)]
     b_copies = [send(group_b, group_b, at_z(d)) for d in z_far]
 
-    arrive([w_core])
-    both = wl[k] + wc[...]
-    for j in range(n_q):
-        w1[j] = jnp.concatenate([both[j * wrows : (j + 1) * wrows], both[TILE:]], axis=0)
-    wx_copies = [send(w1.at[lax.rem(q + d, n_q)], wx.at[d], at_q(d)) for d in q_far]
     arrive(wx_copies)
     summed = w1[q]
     for d in range(1, n_q):
@@ -326,40 +369,64 @@
 
     lax.fori_loop(0, n_src, place_cols, 0)
 
-    b_core = send(bp.at[pl.ds((1 - k) * n_q, n_q)], br, sibling)
+    b_core = {}
+    for d in q_far + [0]:
+        i = lax.rem(q + d, n_q)
+        b_core[d] = send(bp.at[(1 - k) * n_q + i], br.at[i], sibling)
     arrive(wy_copies)
     summed = w2[...]
     for d in range(1, n_y):
         summed = summed + wy[d]
     w3[...] = summed
     wz_copies = [send(w3, wz.at[d], at_z(d)) for d in z_far]
-    arrive([b_core])
-    bs[...] = (bp[pl.ds(k * n_q, n_q)].astype(F32) + br[...].astype(F32)).astype(BF16)
-    back_copies = [send(bs.at[lax.rem(q + d, n_q)], br2.at[d], at_q(d)) for d in q_far]
+    back_copies = []
+    for d in q_far:
+        i = lax.rem(q + d, n_q)
+        arrive([b_core[d]])
+        bs[i] = (bp[k * n_q + i].astype(F32) + br[i].astype(F32)).astype(BF16)
+        back_copies.append(send(bs.at[i], br2.at[d], at_q(d)))
+    arrive([b_core[0]])
+    feature_grad = own_term + (bp[k * n_q + q].astype(F32) + br[q].astype(F32))
 
     arrive(wz_copies)
     summed = w3[...]
     for d in range(1, n_z):
         summed = summed + wz[d]
     summed = summed * scaling
-    bg_o[...] = jnp.sum(summed[wrows:], axis=0, keepdims=True)
     wo[k * n_q + q] = summed[:wrows]
     own_w = wo.at[k * n_q + q]
     wo_copies = [send(own_w, own_w, at_q(d)) for d in q_far]
+    bg_v[...] = jnp.sum(summed[wrows:], axis=0, keepdims=True)
+    put(bg_v, bg_o)
 
     arrive(back_copies)
-    feature_grad = own_term + bs[q].astype(F32)
     for d in range(1, n_q):
         feature_grad = feature_grad + br2[d].astype(F32)
-    fg_o[...] = feature_grad.astype(BF16)
+    fg_v[...] = feature_grad.astype(BF16)
+    put(fg_v, fg_o)
 
     arrive(wo_copies)
     own_half = wo.at[pl.ds(k * n_q, n_q)]
-    arrive([send(own_half, own_half, sibling)])
-    sg_o[...] = wo[pl.ds(0, n_q)].reshape(TILE, TILE)
-    ng_o[...] = wo[pl.ds(n_q, n_q)].reshape(TILE, TILE)
+    last = send(own_half, own_half, sibling)
+    arrive([last])
+    put(wo.at[pl.ds(0, n_q)], sg_o)
+    put(wo.at[pl.ds(n_q, n_q)], ng_o)
+    for copy in local_out:
+        copy.wait()
     for copy in started:
         copy.wait_send()
+
+
+def hand_over(*refs):
+    sources, results, sems = refs[:5], refs[5:10], refs[10]
+    copies = [
+        pltpu.make_async_copy(source, result, sems.at[i])
+        for i, (source, result) in enumerate(zip(sources, results))
+    ]
+    for copy in copies:
+        copy.start()
+    for copy in copies:
+        copy.wait()
 
 
 def on_device(
@@ -382,8 +449,20 @@
     sizes = (n_q, n_y, n_z, slots, scaling)
     wrows = TILE // n_q
     n_dst, n_src = n_col, n_row
-    copies = 7 * (n_y - 1) + 6 * (n_z - 1) + 4 * (n_q - 1) + 4
+    copies = 6 * (n_y - 1) + 6 * (n_z - 1) + 4 * (n_q - 1) + 2 * n_q + 2
     scratch = [
+        pltpu.VMEM((TILE, TILE), BF16),
+        pltpu.VMEM((TILE, TILE), BF16),
+        pltpu.VMEM((TILE, TILE), BF16),
+        pltpu.VMEM((TILE, TILE), BF16),
+        pltpu.VMEM((1, TILE), F32),
+        pltpu.VMEM((1, slots), jnp.int32),
+        pltpu.VMEM((1, slots), jnp.int32),
+        pltpu.VMEM((slots, TILE), jnp.int32),
+        pltpu.VMEM((slots, TILE), jnp.int32),
+        pltpu.VMEM((TILE, TILE), BF16),
+        pltpu.VMEM((TILE, TILE), BF16),
+        pltpu.VMEM((1, TILE), F32),
         pltpu.VMEM((slots, TILE, TILE), BF16),
         pltpu.VMEM((slots, TILE, TILE), BF16),
         pltpu.VMEM((slots, TILE, TILE), BF16),
@@ -421,22 +500,25 @@
         pltpu.SemaphoreType.DMA((copies,)),
         pltpu.SemaphoreType.DMA((copies,)),
         pltpu.SemaphoreType.DMA,
+        pltpu.SemaphoreType.DMA((9,)),
+        pltpu.SemaphoreType.DMA((5,)),
     ]
-    whole = pl.BlockSpec(memory_space=pltpu.VMEM)
-    act, fg, sg, ng, bg = pl.pallas_call(
+    whole = pl.BlockSpec(memory_space=pl.ANY)
+    out_shape = (
+        jax.ShapeDtypeStruct((TILE, TILE), BF16),
+        jax.ShapeDtypeStruct((TILE, TILE), BF16),
+        jax.ShapeDtypeStruct((n_q, wrows, TILE), F32),
+        jax.ShapeDtypeStruct((n_q, wrows, TILE), F32),
+        jax.ShapeDtypeStruct((1, TILE), F32),
+    )
+    results = pl.pallas_call(
         functools.partial(layer_kernel, sizes),
-        out_shape=(
-            jax.ShapeDtypeStruct((TILE, TILE), BF16),
-            jax.ShapeDtypeStruct((TILE, TILE), BF16),
-            jax.ShapeDtypeStruct((TILE, TILE), F32),
-            jax.ShapeDtypeStruct((TILE, TILE), F32),
-            jax.ShapeDtypeStruct((1, TILE), F32),
-        ),
-        in_specs=[whole] * 9,
+        out_shape=out_shape,
+        in_specs=[pl.BlockSpec(memory_space=pltpu.HBM)] * 9,
         out_specs=(whole,) * 5,
         scratch_shapes=scratch,
         compiler_params=pltpu.CompilerParams(
-            collective_id=0, has_side_effects=True, vmem_limit_bytes=44 * 2**20
+            collective_id=0, has_side_effects=True, vmem_limit_bytes=60 * 2**20
         ),
         name="sage_layer",
     )(
@@ -450,7 +532,15 @@
         edge_targets.reshape(slots, -1),
         edge_sources.reshape(slots, -1),
     )
-    return act, fg, sg, ng, bg.reshape(TILE)
+    act, fg, sg, ng, bg = pl.pallas_call(
+        hand_over,
+        out_shape=out_shape,
+        in_specs=[pl.BlockSpec(memory_space=pltpu.VMEM)] * 5,
+        out_specs=(pl.BlockSpec(memory_space=pltpu.HBM),) * 5,
+        scratch_shapes=[pltpu.SemaphoreType.DMA((5,))],
+        name="hand_over",
+    )(*results)
+    return act, fg, sg.reshape(TILE, TILE), ng.reshape(TILE, TILE), bg.reshape(TILE)
 
 
 def solution(mesh):

time: 103 us -> 92.3 us (0.90)
  local copies, waits for them, and re-layouts: 8.37 us -> 0 us
  Pallas kernels: 93.3 us -> 91.4 us
    unnamed x23 -> x0, local copies, waits for them, and re-layouts: 8.37 us -> none
    pallas_call x1 -> x2, Pallas kernels: 93.3 us -> 91.4 us  [the longest x1 89.8 us: on_device(): pl.pallas_call(functools.partial(layer_kernel, sizes), out_shape=out_shap...]
where the time goes in v2:
time: 92.3 us; the launch traced here: 92.1 us
  Pallas kernels  91.4 us (99%)
    pallas_call x1, Pallas kernels, on_device(): pl.pallas_call(functools.partial(layer_kernel, sizes), out_shape=out_shap...  89.8 us

profile of v2, /device:TPU:1, one launch (start us, length us, event | category | flops | bytes accessed | tf_op | source)
XLA Modules:
  0.0 92.1 jit_solution(7543294691016684482)
XLA Ops:
  0.6 89.8 %sage_layer.1 = (bf16[128,128]{1,0:T(8,128)(2,1)}, bf16[128,128]{1,0:T(8,128)(2,1)}, f32[8,16,128]{2,1,0:T(8,128)}, f32[8,16,128]{2,1,0:T(8,128)}, f32[1,128]{1,0:T(1,128)}) custom-call(bf16[128,128]{1,0:T(8,128)(2,1)} %feat_h.1, bf16[128,128]{1,0:T(8,128)(2,1)} %cot_h.1, bf16[128,128]{1,0:T(8,128)(2,1)} %ws_h.1, bf16[128,128]{1,0:T(8,128)(2,1)} %wn_h.1, ...), custom_call_target="tpu_custom_call" | custom-call | tf_op jit(solution)/shard_map/sage_layer/pallas_call | solution.py:514
  90.4 1.6 %hand_over.1 = (bf16[128,128]{1,0:T(8,128)(2,1)}, bf16[128,128]{1,0:T(8,128)(2,1)}, f32[8,16,128]{2,1,0:T(8,128)}, f32[8,16,128]{2,1,0:T(8,128)}, f32[1,128]{1,0:T(1,128)}) custom-call(bf16[128,128]{1,0:T(8,128)(2,1)} %get-tuple-element.15.refs_0_, bf16[128,128]{1,0:T(8,128)(2,1)} %get-tuple-element.16.refs_1_, f32[8,16,128]{2,1,0:T(8,128)} %get-tuple-element.17.refs_2_, ...), custom_call_target="tpu_custom_call" | custom-call | tf_op jit(solution)/shard_map/hand_over/pallas_call | solution.py:535

commit v3 on v2

--- a/solution.py
+++ b/solution.py
@@ -10,7 +10,7 @@
 TILE = 128
 HALF = TILE // 2
 CORES = 2
-UNROLL = 8
+UNROLL = 16
 MESH = pl.DeviceIdType.MESH
 F32 = jnp.float32
 BF16 = jnp.bfloat16
@@ -134,11 +134,17 @@
 
     y_far, z_far, q_far = far_first(n_y), far_first(n_z), far_first(n_q)
 
+    barrier = pltpu.get_barrier_semaphore()
+    partners = [at_q(d) for d in q_far] + [at_y(d) for d in y_far]
+    partners += [at_z(d) for d in z_far] + [sibling]
+    for partner in partners:
+        pl.semaphore_signal(barrier, inc=1, device_id=partner, device_id_type=MESH)
+
     local_in = []
     for i, (far, near) in enumerate(
         zip(
-            (trow_h, tcol_h, feat_h, et_h, es_h, ws_h, wn_h, bias_h, cot_h),
-            (trow, tcol, feat, et, es, ws, wn, bias, cot),
+            (feat_h, trow_h, tcol_h, et_h, es_h, feat_h, ws_h, wn_h, bias_h, cot_h),
+            (xb.at[k * n_q + q], trow, tcol, et, es, feat, ws, wn, bias, cot),
         )
     ):
         local_in.append(pltpu.make_async_copy(far, near, in_sems.at[i]))
@@ -151,13 +157,12 @@
         copy.start()
         local_out.append(copy)
 
-    barrier = pltpu.get_barrier_semaphore()
-    partners = [at_y(d) for d in y_far] + [at_z(d) for d in z_far]
-    partners += [at_q(d) for d in q_far] + [sibling]
-    for partner in partners:
-        pl.semaphore_signal(barrier, inc=1, device_id=partner, device_id_type=MESH)
-
-    for copy in local_in[:2]:
+    pl.semaphore_wait(barrier, len(partners))
+
+    mine = xb.at[k * n_q + q]
+    x_copies = {d: send(feat_h, mine, at_q(d)) for d in q_far}
+    x_core = [send(feat_h, mine, sibling)]
+    for copy in local_in:
         copy.wait()
 
     sub = lax.broadcasted_iota(jnp.int32, (TILE, TILE), 0)
@@ -184,15 +189,6 @@
     meta_copy = pltpu.make_async_copy(meta_v, meta_s, meta_sem)
     meta_copy.start()
 
-    local_in[2].wait()
-    xb[k * n_q + q] = feat[...]
-    pl.semaphore_wait(barrier, len(partners))
-
-    mine = xb.at[k * n_q + q]
-    x_copies = {d: send(mine, mine, at_q(d)) for d in q_far}
-    x_core = [send(mine, mine, sibling)]
-    for copy in local_in[3:]:
-        copy.wait()
 
     def build(g, _):
         base = pl.multiple_of(g * UNROLL, UNROLL)
@@ -212,6 +208,11 @@
 
     lax.fori_loop(0, slots // UNROLL, build, 0)
 
+    for d in reversed(q_far):
+        arrive([x_copies[d]])
+        block = xb.at[k * n_q + lax.rem(q + n_q - d, n_q)]
+        x_core.append(send(block, block, sibling))
+
     tile_sub = lax.broadcasted_iota(jnp.int32, (n_y * 8, TILE), 0)
     wanted = (tile_sub // 8) * n_z + tile_sub % 8
     hits = (jnp.broadcast_to(trow[...], (n_y * 8, TILE)) == wanted) & (tile_sub % 8 < n_z)
@@ -225,10 +226,6 @@
     self_term = jnp.dot(feat[...], ws[...], preferred_element_type=F32)
 
     meta_copy.wait()
-    for d in reversed(q_far):
-        arrive([x_copies[d]])
-        block = xb.at[k * n_q + lax.rem(q + n_q - d, n_q)]
-        x_core.append(send(block, block, sibling))
     arrive(x_core)
 
     def forward(g, acc):
@@ -312,8 +309,6 @@
     b_copies = [send(own_b, own_b, at_y(d)) for d in y_far]
     a_copies = [send(own_a, own_a, at_z(d)) for d in z_far]
 
-    act_v[...] = (preact * sigma).astype(BF16)
-    put(act_v, act_o)
     self_local = lax.dot_general(feat[...], grad_pre, ROWS, preferred_element_type=F32)
     neighbour_local = lax.dot_general(aggregate, grad_pre, ROWS, preferred_element_type=F32)
     bias_local = jnp.sum(grad_pre.astype(F32).reshape(TILE // 8, 8, TILE), axis=0)
@@ -321,8 +316,10 @@
     wl[1, :TILE] = neighbour_local
     wl[0, TILE:] = bias_local
     wl[1, TILE:] = bias_local
+    w_core = send(wl.at[1 - k], wc, sibling)
+    act_v[...] = (preact * sigma).astype(BF16)
+    put(act_v, act_o)
     own_term = lax.dot_general(grad_pre, ws[...], LANES, preferred_element_type=F32)
-    w_core = send(wl.at[1 - k], wc, sibling)
 
     arrive([w_core])
     both = wl[k] + wc[...]
@@ -342,7 +339,13 @@
     for d in range(1, n_q):
         summed = summed + wx[d]
     w2[...] = summed
-    wy_copies = [send(w2, wy.at[d], at_y(d)) for d in y_far]
+    wz_copies = [send(w2, wz.at[d], at_z(d)) for d in z_far]
+    arrive(wz_copies)
+    summed = w2[...]
+    for d in range(1, n_z):
+        summed = summed + wz[d]
+    w3[...] = summed
+    wy_copies = [send(w3, wy.at[d], at_y(d)) for d in y_far]
 
     arrive(a_copies)
     arrive(b_copies)
@@ -374,11 +377,17 @@
         i = lax.rem(q + d, n_q)
         b_core[d] = send(bp.at[(1 - k) * n_q + i], br.at[i], sibling)
     arrive(wy_copies)
-    summed = w2[...]
+    summed = w3[...]
     for d in range(1, n_y):
         summed = summed + wy[d]
-    w3[...] = summed
-    wz_copies = [send(w3, wz.at[d], at_z(d)) for d in z_far]
+    summed = summed * scaling
+    wo[k * n_q + q] = summed[:wrows]
+    own_w = wo.at[k * n_q + q]
+    wo_copies = {d: send(own_w, own_w, at_q(d)) for d in q_far}
+    wo_core = [send(own_w, own_w, sibling)]
+    bg_v[...] = jnp.sum(summed[wrows:], axis=0, keepdims=True)
+    put(bg_v, bg_o)
+
     back_copies = []
     for d in q_far:
         i = lax.rem(q + d, n_q)
@@ -388,27 +397,16 @@
     arrive([b_core[0]])
     feature_grad = own_term + (bp[k * n_q + q].astype(F32) + br[q].astype(F32))
 
-    arrive(wz_copies)
-    summed = w3[...]
-    for d in range(1, n_z):
-        summed = summed + wz[d]
-    summed = summed * scaling
-    wo[k * n_q + q] = summed[:wrows]
-    own_w = wo.at[k * n_q + q]
-    wo_copies = [send(own_w, own_w, at_q(d)) for d in q_far]
-    bg_v[...] = jnp.sum(summed[wrows:], axis=0, keepdims=True)
-    put(bg_v, bg_o)
-
+    for d in reversed(q_far):
+        arrive([wo_copies[d]])
+        block = wo.at[k * n_q + lax.rem(q + n_q - d, n_q)]
+        wo_core.append(send(block, block, sibling))
     arrive(back_copies)
     for d in range(1, n_q):
         feature_grad = feature_grad + br2[d].astype(F32)
     fg_v[...] = feature_grad.astype(BF16)
     put(fg_v, fg_o)
-
-    arrive(wo_copies)
-    own_half = wo.at[pl.ds(k * n_q, n_q)]
-    last = send(own_half, own_half, sibling)
-    arrive([last])
+    arrive(wo_core)
     put(wo.at[pl.ds(0, n_q)], sg_o)
     put(wo.at[pl.ds(n_q, n_q)], ng_o)
     for copy in local_out:
@@ -449,7 +447,7 @@
     sizes = (n_q, n_y, n_z, slots, scaling)
     wrows = TILE // n_q
     n_dst, n_src = n_col, n_row
-    copies = 6 * (n_y - 1) + 6 * (n_z - 1) + 4 * (n_q - 1) + 2 * n_q + 2
+    copies = 6 * (n_y - 1) + 6 * (n_z - 1) + 4 * (n_q - 1) + 3 * n_q + 1
     scratch = [
         pltpu.VMEM((TILE, TILE), BF16),
         pltpu.VMEM((TILE, TILE), BF16),
@@ -500,7 +498,7 @@
         pltpu.SemaphoreType.DMA((copies,)),
         pltpu.SemaphoreType.DMA((copies,)),
         pltpu.SemaphoreType.DMA,
-        pltpu.SemaphoreType.DMA((9,)),
+        pltpu.SemaphoreType.DMA((10,)),
         pltpu.SemaphoreType.DMA((5,)),
     ]
     whole = pl.BlockSpec(memory_space=pl.ANY)

time: 92.3 us -> 88.7 us (0.961)
  Pallas kernels: 91.4 us -> 87.9 us
    pallas_call x1, Pallas kernels: 89.8 us -> 86.2 us  [on_device(): pl.pallas_call(functools.partial(layer_kernel, sizes), out_shape=out_shap...]
where the time goes in v3:
time: 88.7 us; the launch traced here: 88.5 us
  Pallas kernels  87.9 us (99%)
    pallas_call x1, Pallas kernels, on_device(): pl.pallas_call(functools.partial(layer_kernel, sizes), out_shape=out_shap...  86.2 us

profile of v3, /device:TPU:1, one launch (start us, length us, event | category | flops | bytes accessed | tf_op | source)
XLA Modules:
  0.0 88.5 jit_solution(4148779930954687187)
XLA Ops:
  0.6 86.2 %sage_layer.1 = (bf16[128,128]{1,0:T(8,128)(2,1)}, bf16[128,128]{1,0:T(8,128)(2,1)}, f32[8,16,128]{2,1,0:T(8,128)}, f32[8,16,128]{2,1,0:T(8,128)}, f32[1,128]{1,0:T(1,128)}) custom-call(bf16[128,128]{1,0:T(8,128)(2,1)} %feat_h.1, bf16[128,128]{1,0:T(8,128)(2,1)} %cot_h.1, bf16[128,128]{1,0:T(8,128)(2,1)} %ws_h.1, bf16[128,128]{1,0:T(8,128)(2,1)} %wn_h.1, ...), custom_call_target="tpu_custom_call" | custom-call | tf_op jit(solution)/shard_map/sage_layer/pallas_call | solution.py:512
  86.9 1.6 %hand_over.1 = (bf16[128,128]{1,0:T(8,128)(2,1)}, bf16[128,128]{1,0:T(8,128)(2,1)}, f32[8,16,128]{2,1,0:T(8,128)}, f32[8,16,128]{2,1,0:T(8,128)}, f32[1,128]{1,0:T(1,128)}) custom-call(bf16[128,128]{1,0:T(8,128)(2,1)} %get-tuple-element.15.refs_0_, bf16[128,128]{1,0:T(8,128)(2,1)} %get-tuple-element.16.refs_1_, f32[8,16,128]{2,1,0:T(8,128)} %get-tuple-element.17.refs_2_, ...), custom_call_target="tpu_custom_call" | custom-call | tf_op jit(solution)/shard_map/hand_over/pallas_call | solution.py:533

commit v4 on v3

--- a/solution.py
+++ b/solution.py
@@ -47,9 +47,6 @@
     tcol,
     et,
     es,
-    act_v,
-    fg_v,
-    bg_v,
     fwd_adj,
     bwd_adj,
     runs,
@@ -88,7 +85,6 @@
     recv_sems,
     meta_sem,
     in_sems,
-    out_sems,
 ):
     n_q, n_y, n_z, slots, scaling = sizes
     r = lax.axis_index("row")
@@ -97,7 +93,7 @@
     y, z = c // n_z, c % n_z
     n_src = n_q * CORES
     n_dst = n_y * n_z
-    wrows = TILE // n_q
+    wrows = TILE // n_y
 
     def at_y(d):
         return (r, lax.rem(y + d, n_y) * n_z + z)
@@ -149,13 +145,6 @@
     ):
         local_in.append(pltpu.make_async_copy(far, near, in_sems.at[i]))
         local_in[-1].start()
-
-    local_out = []
-
-    def put(src, dst):
-        copy = pltpu.make_async_copy(src, dst, out_sems.at[len(local_out)])
-        copy.start()
-        local_out.append(copy)
 
     pl.semaphore_wait(barrier, len(partners))
 
@@ -317,15 +306,14 @@
     wl[0, TILE:] = bias_local
     wl[1, TILE:] = bias_local
     w_core = send(wl.at[1 - k], wc, sibling)
-    act_v[...] = (preact * sigma).astype(BF16)
-    put(act_v, act_o)
+    act_o[...] = (preact * sigma).astype(BF16)
     own_term = lax.dot_general(grad_pre, ws[...], LANES, preferred_element_type=F32)
 
     arrive([w_core])
     both = wl[k] + wc[...]
-    for j in range(n_q):
+    for j in range(n_y):
         w1[j] = jnp.concatenate([both[j * wrows : (j + 1) * wrows], both[TILE:]], axis=0)
-    wx_copies = [send(w1.at[lax.rem(q + d, n_q)], wx.at[d], at_q(d)) for d in q_far]
+    wy_copies = [send(w1.at[lax.rem(y + d, n_y)], wy.at[d], at_y(d)) for d in y_far]
 
     arrive(a_copies)
     group_a = ga.at[pl.ds(y * n_z, n_z)]
@@ -334,10 +322,10 @@
     group_b = gb.at[pl.ds(z * n_y, n_y)]
     b_copies = [send(group_b, group_b, at_z(d)) for d in z_far]
 
-    arrive(wx_copies)
-    summed = w1[q]
-    for d in range(1, n_q):
-        summed = summed + wx[d]
+    arrive(wy_copies)
+    summed = w1[y]
+    for d in range(1, n_y):
+        summed = summed + wy[d]
     w2[...] = summed
     wz_copies = [send(w2, wz.at[d], at_z(d)) for d in z_far]
     arrive(wz_copies)
@@ -345,7 +333,7 @@
     for d in range(1, n_z):
         summed = summed + wz[d]
     w3[...] = summed
-    wy_copies = [send(w3, wy.at[d], at_y(d)) for d in y_far]
+    wx_copies = [send(w3, wx.at[d], at_q(d)) for d in q_far]
 
     arrive(a_copies)
     arrive(b_copies)
@@ -376,18 +364,6 @@
     for d in q_far + [0]:
         i = lax.rem(q + d, n_q)
         b_core[d] = send(bp.at[(1 - k) * n_q + i], br.at[i], sibling)
-    arrive(wy_copies)
-    summed = w3[...]
-    for d in range(1, n_y):
-        summed = summed + wy[d]
-    summed = summed * scaling
-    wo[k * n_q + q] = summed[:wrows]
-    own_w = wo.at[k * n_q + q]
-    wo_copies = {d: send(own_w, own_w, at_q(d)) for d in q_far}
-    wo_core = [send(own_w, own_w, sibling)]
-    bg_v[...] = jnp.sum(summed[wrows:], axis=0, keepdims=True)
-    put(bg_v, bg_o)
-
     back_copies = []
     for d in q_far:
         i = lax.rem(q + d, n_q)
@@ -397,20 +373,28 @@
     arrive([b_core[0]])
     feature_grad = own_term + (bp[k * n_q + q].astype(F32) + br[q].astype(F32))
 
-    for d in reversed(q_far):
+    arrive(wx_copies)
+    summed = w3[...]
+    for d in range(1, n_q):
+        summed = summed + wx[d]
+    summed = summed * scaling
+    wo[k * n_y + y] = summed[:wrows]
+    own_w = wo.at[k * n_y + y]
+    wo_copies = {d: send(own_w, own_w, at_y(d)) for d in y_far}
+    wo_core = [send(own_w, own_w, sibling)]
+    bg_o[...] = jnp.sum(summed[wrows:], axis=0, keepdims=True)
+
+    for d in reversed(y_far):
         arrive([wo_copies[d]])
-        block = wo.at[k * n_q + lax.rem(q + n_q - d, n_q)]
+        block = wo.at[k * n_y + lax.rem(y + n_y - d, n_y)]
         wo_core.append(send(block, block, sibling))
     arrive(back_copies)
     for d in range(1, n_q):
         feature_grad = feature_grad + br2[d].astype(F32)
-    fg_v[...] = feature_grad.astype(BF16)
-    put(fg_v, fg_o)
+    fg_o[...] = feature_grad.astype(BF16)
     arrive(wo_core)
-    put(wo.at[pl.ds(0, n_q)], sg_o)
-    put(wo.at[pl.ds(n_q, n_q)], ng_o)
-    for copy in local_out:
-        copy.wait()
+    sg_o[...] = wo[pl.ds(0, n_y)]
+    ng_o[...] = wo[pl.ds(n_y, n_y)]
     for copy in started:
         copy.wait_send()
 
@@ -445,9 +429,9 @@
     n_y, n_q = n_col // n_z, n_row // CORES
     scaling = float((TILE * n_row * n_col) ** (-0.5))
     sizes = (n_q, n_y, n_z, slots, scaling)
-    wrows = TILE // n_q
+    wrows = TILE // n_y
     n_dst, n_src = n_col, n_row
-    copies = 6 * (n_y - 1) + 6 * (n_z - 1) + 4 * (n_q - 1) + 3 * n_q + 1
+    copies = 7 * (n_y - 1) + 6 * (n_z - 1) + 3 * (n_q - 1) + 2 * n_q + n_y + 1
     scratch = [
         pltpu.VMEM((TILE, TILE), BF16),
         pltpu.VMEM((TILE, TILE), BF16),
@@ -458,9 +442,6 @@
         pltpu.VMEM((1, slots), jnp.int32),
         pltpu.VMEM((slots, TILE), jnp.int32),
         pltpu.VMEM((slots, TILE), jnp.int32),
-        pltpu.VMEM((TILE, TILE), BF16),
-        pltpu.VMEM((TILE, TILE), BF16),
-        pltpu.VMEM((1, TILE), F32),
         pltpu.VMEM((slots, TILE, TILE), BF16),
         pltpu.VMEM((slots, TILE, TILE), BF16),
         pltpu.VMEM((slots, TILE, TILE), BF16),
@@ -488,38 +469,26 @@
         pltpu.VMEM((n_q, TILE, TILE), BF16),
         pltpu.VMEM((CORES, TILE + 8, TILE), F32),
         pltpu.VMEM((TILE + 8, TILE), F32),
-        pltpu.VMEM((n_q, wrows + 8, TILE), F32),
+        pltpu.VMEM((n_y, wrows + 8, TILE), F32),
         pltpu.VMEM((n_q, wrows + 8, TILE), F32),
         pltpu.VMEM((wrows + 8, TILE), F32),
         pltpu.VMEM((n_y, wrows + 8, TILE), F32),
         pltpu.VMEM((wrows + 8, TILE), F32),
         pltpu.VMEM((n_z, wrows + 8, TILE), F32),
-        pltpu.VMEM((CORES * n_q, wrows, TILE), F32),
+        pltpu.VMEM((CORES * n_y, wrows, TILE), F32),
         pltpu.SemaphoreType.DMA((copies,)),
         pltpu.SemaphoreType.DMA((copies,)),
         pltpu.SemaphoreType.DMA,
         pltpu.SemaphoreType.DMA((10,)),
-        pltpu.SemaphoreType.DMA((5,)),
     ]
-    whole = pl.BlockSpec(memory_space=pl.ANY)
     out_shape = (
         jax.ShapeDtypeStruct((TILE, TILE), BF16),
         jax.ShapeDtypeStruct((TILE, TILE), BF16),
-        jax.ShapeDtypeStruct((n_q, wrows, TILE), F32),
-        jax.ShapeDtypeStruct((n_q, wrows, TILE), F32),
+        jax.ShapeDtypeStruct((n_y, wrows, TILE), F32),
+        jax.ShapeDtypeStruct((n_y, wrows, TILE), F32),
         jax.ShapeDtypeStruct((1, TILE), F32),
     )
-    results = pl.pallas_call(
-        functools.partial(layer_kernel, sizes),
-        out_shape=out_shape,
-        in_specs=[pl.BlockSpec(memory_space=pltpu.HBM)] * 9,
-        out_specs=(whole,) * 5,
-        scratch_shapes=scratch,
-        compiler_params=pltpu.CompilerParams(
-            collective_id=0, has_side_effects=True, vmem_limit_bytes=60 * 2**20
-        ),
-        name="sage_layer",
-    )(
+    operands = (
         features,
         cotangent,
         self_weight,
@@ -530,12 +499,25 @@
         edge_targets.reshape(slots, -1),
         edge_sources.reshape(slots, -1),
     )
+    operands = [pltpu.with_memory_space_constraint(v, pltpu.HBM) for v in operands]
+    results = pl.pallas_call(
+        functools.partial(layer_kernel, sizes),
+        out_shape=out_shape,
+        in_specs=[pl.BlockSpec(memory_space=pltpu.HBM)] * 9,
+        out_specs=(pl.BlockSpec(memory_space=pltpu.VMEM),) * 5,
+        scratch_shapes=scratch,
+        compiler_params=pltpu.CompilerParams(
+            collective_id=0, has_side_effects=True, vmem_limit_bytes=44 * 2**20
+        ),
+        name="sage_layer",
+    )(*operands)
     act, fg, sg, ng, bg = pl.pallas_call(
         hand_over,
         out_shape=out_shape,
         in_specs=[pl.BlockSpec(memory_space=pltpu.VMEM)] * 5,
         out_specs=(pl.BlockSpec(memory_space=pltpu.HBM),) * 5,
         scratch_shapes=[pltpu.SemaphoreType.DMA((5,))],
+        compiler_params=pltpu.CompilerParams(vmem_limit_bytes=2 * 2**20),
         name="hand_over",
     )(*results)
     return act, fg, sg.reshape(TILE, TILE), ng.reshape(TILE, TILE), bg.reshape(TILE)

time: 88.7 us -> 84.2 us (0.949)
  Pallas kernels: 87.9 us -> 83.4 us
    pallas_call x1, Pallas kernels: 86.2 us -> 82.7 us  [on_device(): pl.pallas_call(functools.partial(layer_kernel, sizes), out_shape=out_shap...]
    pallas_call x1, Pallas kernels: 1.63 us -> 0.72 us  [on_device(): pl.pallas_call(hand_over, out_shape=out_shape, in_specs=[pl.BlockSpec(mem...]
where the time goes in v4:
time: 84.2 us; the launch traced here: 84.1 us
  Pallas kernels  83.4 us (99%)
    pallas_call x1, Pallas kernels, on_device(): pl.pallas_call(functools.partial(layer_kernel, sizes), out_shape=out_shap...  82.7 us

profile of v4, /device:TPU:1, one launch (start us, length us, event | category | flops | bytes accessed | tf_op | source)
XLA Modules:
  0.0 84.1 jit_solution(14928234262460926109)
XLA Ops:
  0.6 82.7 %sage_layer.1 = (bf16[128,128]{1,0:T(8,128)(2,1)S(1)}, bf16[128,128]{1,0:T(8,128)(2,1)S(1)}, f32[8,16,128]{2,1,0:T(8,128)S(1)}, f32[8,16,128]{2,1,0:T(8,128)S(1)}, f32[1,128]{1,0:T(1,128)S(1)}) custom-call(bf16[128,128]{1,0:T(8,128)(2,1)} %feat_h.1, bf16[128,128]{1,0:T(8,128)(2,1)} %cot_h.1, bf16[128,128]{1,0:T(8,128)(2,1)} %ws_h.1, bf16[128,128]{1,0:T(8,128)(2,1)} %wn_h.1, ...), custom_call_target="tpu_custom_call" | custom-call | tf_op jit(solution)/shard_map/sage_layer/pallas_call | solution.py:503
  83.4 0.7 hand_over.1

commit v5 on v4

--- a/solution.py
+++ b/solution.py
@@ -11,6 +11,7 @@
 HALF = TILE // 2
 CORES = 2
 UNROLL = 16
+STRETCH = 64
 MESH = pl.DeviceIdType.MESH
 F32 = jnp.float32
 BF16 = jnp.bfloat16
@@ -101,8 +102,18 @@
     def at_z(d):
         return (r, y * n_z + lax.rem(z + d, n_z))
 
+    n_x = n_q // 2
+    x, h = q // 2, q % 2
+    q_steps = [(dx, dh) for dx in range(n_x) for dh in range(2)]
+
+    def q_to(d):
+        return lax.rem(x + q_steps[d][0], n_x) * 2 + lax.rem(h + q_steps[d][1], 2)
+
+    def q_from(d):
+        return lax.rem(x + n_x - q_steps[d][0], n_x) * 2 + lax.rem(h + q_steps[d][1], 2)
+
     def at_q(d):
-        return (lax.rem(q + d, n_q) * CORES + k, c)
+        return (q_to(d) * CORES + k, c)
 
     sibling = (q * CORES + 1 - k, c)
 
@@ -128,7 +139,11 @@
         for copy in copies:
             copy.wait_recv()
 
-    y_far, z_far, q_far = far_first(n_y), far_first(n_z), far_first(n_q)
+    y_far, z_far = far_first(n_y), far_first(n_z)
+    q_far = sorted(
+        range(1, n_q),
+        key=lambda d: -min(q_steps[d][0], n_x - q_steps[d][0]) - 4 * q_steps[d][1],
+    )
 
     barrier = pltpu.get_barrier_semaphore()
     partners = [at_q(d) for d in q_far] + [at_y(d) for d in y_far]
@@ -199,7 +214,7 @@
 
     for d in reversed(q_far):
         arrive([x_copies[d]])
-        block = xb.at[k * n_q + lax.rem(q + n_q - d, n_q)]
+        block = xb.at[k * n_q + q_from(d)]
         x_core.append(send(block, block, sibling))
 
     tile_sub = lax.broadcasted_iota(jnp.int32, (n_y * 8, TILE), 0)
@@ -218,8 +233,8 @@
     arrive(x_core)
 
     def forward(g, acc):
-        for u in range(UNROLL):
-            s = g * UNROLL + u
+        for u in range(STRETCH):
+            s = g * STRETCH + u
             word = meta_s[0, s]
             slot, col = word & 127, (word >> 7) & 31
             source = xb[(col & 1) * n_q + (col >> 1)]
@@ -228,7 +243,7 @@
             runs[s] = acc.astype(BF16)
         return acc
 
-    lax.fori_loop(0, slots // UNROLL, forward, jnp.zeros((TILE, TILE), F32))
+    lax.fori_loop(0, slots // STRETCH, forward, jnp.zeros((TILE, TILE), F32))
 
     def place_rows(i, _):
         word = meta_s[1, i]
@@ -339,8 +354,8 @@
     arrive(b_copies)
 
     def backward(g, acc):
-        for u in range(UNROLL):
-            s = g * UNROLL + u
+        for u in range(STRETCH):
+            s = g * STRETCH + u
             word = meta_s[2, s]
             slot, row = word & 127, (word >> 7) & 31
             target = jnp.concatenate([ga[row], gb[(row % n_z) * n_y + row // n_z]], axis=0)
@@ -349,7 +364,7 @@
             runs[s] = acc.astype(BF16)
         return acc
 
-    lax.fori_loop(0, slots // UNROLL, backward, jnp.zeros((TILE, TILE), F32))
+    lax.fori_loop(0, slots // STRETCH, backward, jnp.zeros((TILE, TILE), F32))
 
     def place_cols(j, _):
         word = meta_s[3, j]
@@ -362,11 +377,11 @@
 
     b_core = {}
     for d in q_far + [0]:
-        i = lax.rem(q + d, n_q)
+        i = q_to(d)
         b_core[d] = send(bp.at[(1 - k) * n_q + i], br.at[i], sibling)
     back_copies = []
     for d in q_far:
-        i = lax.rem(q + d, n_q)
+        i = q_to(d)
         arrive([b_core[d]])
         bs[i] = (bp[k * n_q + i].astype(F32) + br[i].astype(F32)).astype(BF16)
         back_copies.append(send(bs.at[i], br2.at[d], at_q(d)))

time: 84.2 us -> 83.5 us (level)
  no operation moved by 1% of the time
where the time goes in v5:
time: 83.5 us; the launch traced here: 83.3 us
  Pallas kernels  82.7 us (99%)
    pallas_call x1, Pallas kernels, on_device(): pl.pallas_call(functools.partial(layer_kernel, sizes), out_shape=out_shap...  82 us

profile of v5, /device:TPU:1, one launch (start us, length us, event | category | flops | bytes accessed | tf_op | source)
XLA Modules:
  0.0 83.3 jit_solution(6144516253255603530)
XLA Ops:
  0.6 82.0 %sage_layer.1 = (bf16[128,128]{1,0:T(8,128)(2,1)S(1)}, bf16[128,128]{1,0:T(8,128)(2,1)S(1)}, f32[8,16,128]{2,1,0:T(8,128)S(1)}, f32[8,16,128]{2,1,0:T(8,128)S(1)}, f32[1,128]{1,0:T(1,128)S(1)}) custom-call(bf16[128,128]{1,0:T(8,128)(2,1)} %feat_h.1, bf16[128,128]{1,0:T(8,128)(2,1)} %cot_h.1, bf16[128,128]{1,0:T(8,128)(2,1)} %ws_h.1, bf16[128,128]{1,0:T(8,128)(2,1)} %wn_h.1, ...), custom_call_target="tpu_custom_call" | custom-call | tf_op jit(solution)/shard_map/sage_layer/pallas_call | solution.py:518
  82.6 0.7 hand_over.1

commit v6 on v5

--- a/solution.py
+++ b/solution.py
@@ -11,7 +11,7 @@
 HALF = TILE // 2
 CORES = 2
 UNROLL = 16
-STRETCH = 64
+STRETCH = 32
 MESH = pl.DeviceIdType.MESH
 F32 = jnp.float32
 BF16 = jnp.bfloat16
@@ -73,14 +73,22 @@
     br,
     bs,
     br2,
+    b0,
+    b1,
+    by,
+    b2,
+    bc,
     wl,
     wc,
+    w0,
     w1,
     wx,
     w2,
     wy,
     w3,
     wz,
+    w4,
+    wh,
     wo,
     send_sems,
     recv_sems,
@@ -245,15 +253,16 @@
 
     lax.fori_loop(0, slots // STRETCH, forward, jnp.zeros((TILE, TILE), F32))
 
-    def place_rows(i, _):
-        word = meta_s[1, i]
-        run = runs[word & 127]
-        run = jnp.where(word >= 256, run, jnp.zeros_like(run))
-        pa[i] = run[:HALF]
-        pb[(i % n_z) * n_y + i // n_z] = run[HALF:]
+    def place_rows(yy, _):
+        for zz in range(n_z):
+            word = meta_s[1, yy * n_z + zz]
+            run = runs[word & 127]
+            run = jnp.where(word >= 256, run, jnp.zeros_like(run))
+            pa[yy * n_z + zz] = run[:HALF]
+            pb[zz * n_y + yy] = run[HALF:]
         return 0
 
-    lax.fori_loop(0, n_dst, place_rows, 0)
+    lax.fori_loop(0, n_y, place_rows, 0)
 
     a_copies = [
         send(pa.at[pl.ds(lax.rem(y + d, n_y) * n_z, n_z)], ra.at[d], at_y(d)) for d in y_far
@@ -269,9 +278,15 @@
     deg2[...] = summed
     deg2_copies = [send(deg2, deg2_r.at[d], at_z(d)) for d in z_far]
 
-    arrive(a_copies)
+    total = pb[pl.ds(z * n_y, n_y)].astype(F32)
+    for d, copy in zip(z_far, b_copies):
+        arrive([copy])
+        total = total + rb[d].astype(F32)
+    sb[...] = total.astype(BF16)
+    b2_copies = [send(sb.at[lax.rem(y + d, n_y)], rb2.at[d], at_y(d)) for d in y_far]
     total = pa[pl.ds(y * n_z, n_z)].astype(F32)
-    for d in range(1, n_y):
+    for d, copy in zip(y_far, a_copies):
+        arrive([copy])
         total = total + ra[d].astype(F32)
     sa[...] = total.astype(BF16)
     a2_copies = [send(sa.at[lax.rem(z + d, n_z)], ra2.at[d], at_z(d)) for d in z_far]
@@ -284,12 +299,6 @@
     degree = jnp.sum(jnp.where(sub8 == z, degree, 0.0), axis=0, keepdims=True)
     inverse = 1.0 / (jnp.broadcast_to(degree, (TILE, TILE)).T + 1.0)
 
-    arrive(b_copies)
-    total = pb[pl.ds(z * n_y, n_y)].astype(F32)
-    for d in range(1, n_z):
-        total = total + rb[d].astype(F32)
-    sb[...] = total.astype(BF16)
-    b2_copies = [send(sb.at[lax.rem(y + d, n_y)], rb2.at[d], at_y(d)) for d in y_far]
     arrive(a2_copies)
     upper = sa[z].astype(F32)
     for d in range(1, n_z):
@@ -316,18 +325,16 @@
     self_local = lax.dot_general(feat[...], grad_pre, ROWS, preferred_element_type=F32)
     neighbour_local = lax.dot_general(aggregate, grad_pre, ROWS, preferred_element_type=F32)
     bias_local = jnp.sum(grad_pre.astype(F32).reshape(TILE // 8, 8, TILE), axis=0)
-    wl[0, :TILE] = self_local
-    wl[1, :TILE] = neighbour_local
-    wl[0, TILE:] = bias_local
-    wl[1, TILE:] = bias_local
+    wl[0] = self_local
+    wl[1] = neighbour_local
     w_core = send(wl.at[1 - k], wc, sibling)
+    b0[...] = bias_local
     act_o[...] = (preact * sigma).astype(BF16)
     own_term = lax.dot_general(grad_pre, ws[...], LANES, preferred_element_type=F32)
 
     arrive([w_core])
-    both = wl[k] + wc[...]
-    for j in range(n_y):
-        w1[j] = jnp.concatenate([both[j * wrows : (j + 1) * wrows], both[TILE:]], axis=0)
+    w0[...] = (wl[k] + wc[...]).reshape(n_y, wrows, TILE)
+    w1[...] = w0[...].astype(BF16)
     wy_copies = [send(w1.at[lax.rem(y + d, n_y)], wy.at[d], at_y(d)) for d in y_far]
 
     arrive(a_copies)
@@ -338,20 +345,26 @@
     b_copies = [send(group_b, group_b, at_z(d)) for d in z_far]
 
     arrive(wy_copies)
-    summed = w1[y]
+    summed = w0[y]
     for d in range(1, n_y):
-        summed = summed + wy[d]
-    w2[...] = summed
-    wz_copies = [send(w2, wz.at[d], at_z(d)) for d in z_far]
+        summed = summed + wy[d].astype(F32)
+    w2[...] = jnp.concatenate([summed, b0[...]], axis=0)
+    wx_copies = [send(w2, wx.at[d], at_q(2 * d)) for d in range(1, n_x)]
+    arrive(wx_copies)
+    summed = w2[...]
+    for d in range(1, n_x):
+        summed = summed + wx[d]
+    w3[...] = summed
+    wz_copies = [send(w3, wz.at[d], at_z(d)) for d in z_far]
+
+    arrive(a_copies)
+    arrive(b_copies)
     arrive(wz_copies)
-    summed = w2[...]
+    summed = w3[...]
     for d in range(1, n_z):
         summed = summed + wz[d]
-    w3[...] = summed
-    wx_copies = [send(w3, wx.at[d], at_q(d)) for d in q_far]
-
-    arrive(a_copies)
-    arrive(b_copies)
+    w4[...] = summed
+    w_flip = send(w4, wh, at_q(1))
 
     def backward(g, acc):
         for u in range(STRETCH):
@@ -366,14 +379,15 @@
 
     lax.fori_loop(0, slots // STRETCH, backward, jnp.zeros((TILE, TILE), F32))
 
-    def place_cols(j, _):
-        word = meta_s[3, j]
-        run = runs[word & 127]
-        run = jnp.where(word >= 256, run, jnp.zeros_like(run))
-        bp[(j % CORES) * n_q + j // CORES] = run
+    def place_cols(g, _):
+        for u in range(4):
+            word = meta_s[3, g * 4 + u]
+            run = runs[word & 127]
+            run = jnp.where(word >= 256, run, jnp.zeros_like(run))
+            bp[(u % CORES) * n_q + g * 2 + u // CORES] = run
         return 0
 
-    lax.fori_loop(0, n_src, place_cols, 0)
+    lax.fori_loop(0, n_src // 4, place_cols, 0)
 
     b_core = {}
     for d in q_far + [0]:
@@ -388,30 +402,37 @@
     arrive([b_core[0]])
     feature_grad = own_term + (bp[k * n_q + q].astype(F32) + br[q].astype(F32))
 
-    arrive(wx_copies)
-    summed = w3[...]
-    for d in range(1, n_q):
-        summed = summed + wx[d]
-    summed = summed * scaling
+    arrive([w_flip])
+    summed = (w4[...] + wh[...]) * scaling
     wo[k * n_y + y] = summed[:wrows]
     own_w = wo.at[k * n_y + y]
     wo_copies = {d: send(own_w, own_w, at_y(d)) for d in y_far}
     wo_core = [send(own_w, own_w, sibling)]
-    bg_o[...] = jnp.sum(summed[wrows:], axis=0, keepdims=True)
+    b1[...] = summed[wrows:]
+    by_copies = [send(b1, by.at[d], at_y(d)) for d in y_far]
 
     for d in reversed(y_far):
         arrive([wo_copies[d]])
         block = wo.at[k * n_y + lax.rem(y + n_y - d, n_y)]
         wo_core.append(send(block, block, sibling))
-    arrive(back_copies)
-    for d in range(1, n_q):
+    arrive(by_copies)
+    bias_sum = b1[...]
+    for d in range(1, n_y):
+        bias_sum = bias_sum + by[d]
+    b2[...] = bias_sum
+    b_last = send(b2, bc, sibling)
+    for d, copy in zip(q_far, back_copies):
+        arrive([copy])
         feature_grad = feature_grad + br2[d].astype(F32)
     fg_o[...] = feature_grad.astype(BF16)
+    arrive([b_last])
+    bg_o[...] = jnp.sum(b2[...] + bc[...], axis=0, keepdims=True)
     arrive(wo_core)
     sg_o[...] = wo[pl.ds(0, n_y)]
     ng_o[...] = wo[pl.ds(n_y, n_y)]
     for copy in started:
         copy.wait_send()
+    assert used[0] == send_sems.shape[0]
 
 
 def hand_over(*refs):
@@ -446,7 +467,7 @@
     sizes = (n_q, n_y, n_z, slots, scaling)
     wrows = TILE // n_y
     n_dst, n_src = n_col, n_row
-    copies = 7 * (n_y - 1) + 6 * (n_z - 1) + 3 * (n_q - 1) + 2 * n_q + n_y + 1
+    copies = 8 * (n_y - 1) + 6 * (n_z - 1) + 2 * (n_q - 1) + n_q // 2 + 2 * n_q + n_y + 2
     scratch = [
         pltpu.VMEM((TILE, TILE), BF16),
         pltpu.VMEM((TILE, TILE), BF16),
@@ -482,14 +503,22 @@
         pltpu.VMEM((n_q, TILE, TILE), BF16),
         pltpu.VMEM((n_q, TILE, TILE), BF16),
         pltpu.VMEM((n_q, TILE, TILE), BF16),
-        pltpu.VMEM((CORES, TILE + 8, TILE), F32),
-        pltpu.VMEM((TILE + 8, TILE), F32),
-        pltpu.VMEM((n_y, wrows + 8, TILE), F32),
-        pltpu.VMEM((n_q, wrows + 8, TILE), F32),
+        pltpu.VMEM((8, TILE), F32),
+        pltpu.VMEM((8, TILE), F32),
+        pltpu.VMEM((n_y, 8, TILE), F32),
+        pltpu.VMEM((8, TILE), F32),
+        pltpu.VMEM((8, TILE), F32),
+        pltpu.VMEM((CORES, TILE, TILE), F32),
+        pltpu.VMEM((TILE, TILE), F32),
+        pltpu.VMEM((n_y, wrows, TILE), F32),
+        pltpu.VMEM((n_y, wrows, TILE), BF16),
+        pltpu.VMEM((n_q // 2, wrows + 8, TILE), F32),
         pltpu.VMEM((wrows + 8, TILE), F32),
-        pltpu.VMEM((n_y, wrows + 8, TILE), F32),
+        pltpu.VMEM((n_y, wrows, TILE), BF16),
         pltpu.VMEM((wrows + 8, TILE), F32),
         pltpu.VMEM((n_z, wrows + 8, TILE), F32),
+        pltpu.VMEM((wrows + 8, TILE), F32),
+        pltpu.VMEM((wrows + 8, TILE), F32),
         pltpu.VMEM((CORES * n_y, wrows, TILE), F32),
         pltpu.SemaphoreType.DMA((copies,)),
         pltpu.SemaphoreType.DMA((copies,)),

time: 83.5 us -> 79.7 us (0.954)
  Pallas kernels: 82.7 us -> 78.9 us
    pallas_call x1, Pallas kernels: 82 us -> 78.2 us  [on_device(): pl.pallas_call(functools.partial(layer_kernel, sizes), out_shape=out_shap...]
where the time goes in v6:
time: 79.7 us; the launch traced here: 79.5 us
  Pallas kernels  78.9 us (99%)
    pallas_call x1, Pallas kernels, on_device(): pl.pallas_call(functools.partial(layer_kernel, sizes), out_shape=out_shap...  78.2 us

profile of v6, /device:TPU:1, one launch (start us, length us, event | category | flops | bytes accessed | tf_op | source)
XLA Modules:
  0.0 79.5 jit_solution(13826880350372651607)
XLA Ops:
  0.6 78.2 %sage_layer.1 = (bf16[128,128]{1,0:T(8,128)(2,1)S(1)}, bf16[128,128]{1,0:T(8,128)(2,1)S(1)}, f32[8,16,128]{2,1,0:T(8,128)S(1)}, f32[8,16,128]{2,1,0:T(8,128)S(1)}, f32[1,128]{1,0:T(1,128)S(1)}) custom-call(bf16[128,128]{1,0:T(8,128)(2,1)} %feat_h.1, bf16[128,128]{1,0:T(8,128)(2,1)} %cot_h.1, bf16[128,128]{1,0:T(8,128)(2,1)} %ws_h.1, bf16[128,128]{1,0:T(8,128)(2,1)} %wn_h.1, ...), custom_call_target="tpu_custom_call" | custom-call | tf_op jit(solution)/shard_map/sage_layer/pallas_call | solution.py:547
  78.8 0.7 hand_over.1

commit v7 on v6

--- a/solution.py
+++ b/solution.py
@@ -329,8 +329,6 @@
     wl[1] = neighbour_local
     w_core = send(wl.at[1 - k], wc, sibling)
     b0[...] = bias_local
-    act_o[...] = (preact * sigma).astype(BF16)
-    own_term = lax.dot_general(grad_pre, ws[...], LANES, preferred_element_type=F32)
 
     arrive([w_core])
     w0[...] = (wl[k] + wc[...]).reshape(n_y, wrows, TILE)
@@ -343,6 +341,8 @@
     arrive(b_copies)
     group_b = gb.at[pl.ds(z * n_y, n_y)]
     b_copies = [send(group_b, group_b, at_z(d)) for d in z_far]
+    act_o[...] = (preact * sigma).astype(BF16)
+    own_term = lax.dot_general(grad_pre, ws[...], LANES, preferred_element_type=F32)
 
     arrive(wy_copies)
     summed = w0[y]

time: 79.7 us -> 79.7 us (level)
  no operation moved by 1% of the time
where the time goes in v7:
time: 79.7 us; the launch traced here: 79.5 us
  Pallas kernels  78.9 us (99%)
    pallas_call x1, Pallas kernels, on_device(): pl.pallas_call(functools.partial(layer_kernel, sizes), out_shape=out_shap...  78.2 us

profile of v7, /device:TPU:1, one launch (start us, length us, event | category | flops | bytes accessed | tf_op | source)
XLA Modules:
  0.0 79.5 jit_solution(15468607164320100845)
XLA Ops:
  0.6 78.2 %sage_layer.1 = (bf16[128,128]{1,0:T(8,128)(2,1)S(1)}, bf16[128,128]{1,0:T(8,128)(2,1)S(1)}, f32[8,16,128]{2,1,0:T(8,128)S(1)}, f32[8,16,128]{2,1,0:T(8,128)S(1)}, f32[1,128]{1,0:T(1,128)S(1)}) custom-call(bf16[128,128]{1,0:T(8,128)(2,1)} %feat_h.1, bf16[128,128]{1,0:T(8,128)(2,1)} %cot_h.1, bf16[128,128]{1,0:T(8,128)(2,1)} %ws_h.1, bf16[128,128]{1,0:T(8,128)(2,1)} %wn_h.1, ...), custom_call_target="tpu_custom_call" | custom-call | tf_op jit(solution)/shard_map/sage_layer/pallas_call | solution.py:547
  78.8 0.7 hand_over.1
